TPU v7x, 32 devices: a whole 2x2x4 slice. The times are simulated.
32 devices in a mesh: src: 4 (over z), ctx: 8 (over y, x, core).
Axes of the slice: x: 2, y: 2, z: 4, core: 2. Of those that a mesh axis runs over, the one named last changes fastest.
Arguments:
- embeddings: bfloat16 [32768, 1536], P(('src', 'ctx')), may hold values from -6 to 6
- positions: int32 [32768], P(('src', 'ctx')), may hold values from -1 to 16383, as said below
- in_weight: bfloat16 [1536, 768], replicated, may hold values from -0.15625 to 0.15625
- norm_gain: float32 [768], replicated, may hold values from 0.1 to 1.9
- qkv_weight: bfloat16 [768, 3, 768], P(None, None, 'src'), may hold values from -3 to 3
- out_weight: bfloat16 [768, 768], P('src'), may hold values from -0.875 to 0.875
- neighbors: int32 [128, 4], replicated, may hold values from 0 to 127, as said below
- upstream: bfloat16 [16384, 768], P('ctx'), may hold values from -0.125 to 0.125
Outputs:
- encoded: bfloat16 [16384, 768], P('ctx')
- in_grad: float32 [1536, 768], P('ctx', 'src')
- gain_grad: float32 [768], replicated
- qkv_grad: float32 [768, 3, 768], P(None, None, 'src')
- out_grad: float32 [768, 768], P('src')
Inputs may be any that keep to these rules, and one draw needn't show every extreme that they name: Every position 0 to 16383 belongs to exactly one tile; -1 marks a dropped tile. The 1024 tiles of one producer device (consecutive rows) send at most 128 kept tiles to one sequence shard (positions 2048 s to 2048 s + 2047), and every shard receives exactly 128 from some producer device. neighbors[b, 0] = b; entry 1 is a block of b's own shard of 16 consecutive blocks; entry 2 a block of the shard before (of its own for the first shard); entry 3 a block of the shard after (of its own for the last). Entries may repeat.
All inputs are finite; a program needn't handle non-finite values.
Results may differ from a plain program's by a relative error of at most 0.018.
Values may be sent and summed in bfloat16 or wider, within the bound.
A program may use at most 192 MiB of HBM per device.

v0:
```python
import jax
import jax.numpy as jnp
from jax import lax
from jax.sharding import PartitionSpec as P

HEAD = 48
BLOCK = 128
NBR = 4


EPS = 1e-05


def with_halo(cells, sides, width):
    for axis, dim in sides:
        count = lax.axis_size(axis)
        ends = count - 1
        head = lax.slice_in_dim(cells, 0, width, axis=dim)
        tail = lax.slice_in_dim(cells, cells.shape[dim] - width, cells.shape[dim], axis=dim)
        cells = jnp.concatenate(
            [
                lax.ppermute(tail, axis, [(i, (i + 1) % count) for i in range(ends)]),
                cells,
                lax.ppermute(head, axis, [((i + 1) % count, i) for i in range(ends)]),
            ],
            axis=dim,
        )
    return cells


def from_behind(value, axis, steps):
    count = lax.axis_size(axis)
    initial, last = (max(0, -steps), min(count, count - steps))
    return lax.ppermute(value, axis, [(source, source + steps) for source in range(initial, last)])


def as_rounded(values):
    return lax.optimization_barrier(values.astype(jnp.bfloat16)).astype(jnp.float32)


def attend_probs(queries, key_rows):
    num_blocks, block_rows, head_count, head_size = queries.shape
    scores = jnp.einsum("gqhd,gjkhd->ghqjk", queries, key_rows, preferred_element_type=jnp.float32)
    scores = scores.reshape(num_blocks, head_count, block_rows, -1) * HEAD ** (-0.5)
    row_max = jnp.max(scores, -1, keepdims=True)
    powers = jnp.exp(scores - row_max)
    row_sum = jnp.sum(powers, -1, keepdims=True)
    return ((powers / row_sum).astype(jnp.bfloat16), row_max, row_sum)


def local(embeddings, positions, in_weight, norm_gain, qkv_weight, out_weight, neighbors, upstream):
    shards = lax.axis_size("ctx")
    my_shard = lax.axis_index("ctx")
    seq_dev, model_dim = upstream.shape
    per_shard = seq_dev // BLOCK
    produced = positions.shape[0]
    capacity = produced // shards
    target = jnp.floor_divide(positions, seq_dev)
    onehot = (target[:, None] == jnp.arange(shards, dtype=jnp.int32)[None, :]).astype(jnp.int32)
    order_in = jnp.sum((jnp.cumsum(onehot, 0) - onehot) * onehot, 1)
    slot_index = jnp.where(positions >= 0, target * capacity + order_in, produced)
    local_pos = positions - target * seq_dev
    send_rows = (
        jnp.zeros((produced, embeddings.shape[1]), jnp.bfloat16)
        .at[slot_index]
        .set(embeddings, mode="drop")
    )
    send_pos = jnp.full((produced,), -1, jnp.int32).at[slot_index].set(local_pos, mode="drop")
    got_pos = lax.all_to_all(
        send_pos.reshape(shards, capacity), "ctx", split_axis=0, concat_axis=0, tiled=True
    ).reshape(produced)
    got_rows = lax.all_to_all(
        send_rows.reshape(shards, capacity, -1), "ctx", split_axis=0, concat_axis=0, tiled=True
    )
    got_rows = got_rows.reshape(produced, -1)
    is_valid = got_pos >= 0
    target_row = jnp.where(is_valid, got_pos, seq_dev)
    projected = as_rounded(jnp.dot(got_rows, in_weight, preferred_element_type=jnp.float32))
    placed = jnp.zeros((seq_dev, model_dim), jnp.float32).at[target_row].set(projected, mode="drop")
    start_x = lax.psum(placed.astype(jnp.bfloat16), "src")
    x_float = start_x.astype(jnp.float32)
    centred = x_float - jnp.mean(x_float, -1, keepdims=True)
    inv_std = lax.rsqrt(jnp.mean(centred * centred, -1, keepdims=True) + EPS)
    normed = centred * inv_std
    hidden = (normed * norm_gain).astype(jnp.bfloat16)
    local_cols = qkv_weight.shape[2]
    heads_here = local_cols // HEAD
    flat_weight = qkv_weight.reshape(model_dim, 3 * local_cols)
    project = jnp.dot(hidden, flat_weight, preferred_element_type=jnp.float32)
    project = project.astype(jnp.bfloat16).reshape(seq_dev, 3, local_cols)
    ext_kv = with_halo(project[:, 1:], (("ctx", 0),), seq_dev)
    ext_blocks = ext_kv.reshape(3 * per_shard, BLOCK, 2, heads_here, HEAD)
    my_lists = lax.dynamic_slice_in_dim(neighbors, my_shard * per_shard, per_shard, 0)
    ext_index = my_lists - (my_shard - 1) * per_shard
    chosen = ext_blocks[ext_index]
    key_rows = chosen[:, :, :, 0]
    value_rows = chosen[:, :, :, 1]
    queries = project[:, 0].reshape(per_shard, BLOCK, heads_here, HEAD)
    attn_probs, row_max, row_sum = attend_probs(queries, key_rows)
    flat_keys = key_rows.reshape(per_shard, NBR * BLOCK, heads_here, HEAD)
    flat_values = value_rows.reshape(per_shard, NBR * BLOCK, heads_here, HEAD)
    mixed = jnp.einsum(
        "ghqm,gmhd->gqhd", attn_probs, flat_values, preferred_element_type=jnp.float32
    )
    mixed = mixed.astype(jnp.bfloat16).reshape(seq_dev, local_cols)
    partial_out = as_rounded(jnp.dot(mixed, out_weight, preferred_element_type=jnp.float32))
    encoded = (
        x_float + lax.psum(partial_out.astype(jnp.bfloat16), "src").astype(jnp.float32)
    ).astype(jnp.bfloat16)
    d_mixed = lax.dot_general(
        upstream, out_weight, (((1,), (1,)), ((), ())), preferred_element_type=jnp.float32
    ).astype(jnp.bfloat16)
    out_part = lax.dot_general(
        mixed, upstream, (((0,), (0,)), ((), ())), preferred_element_type=jnp.float32
    )
    dout_blocks = d_mixed.reshape(per_shard, BLOCK, heads_here, HEAD)
    prob_grad = jnp.einsum(
        "gqhd,gmhd->ghqm", dout_blocks, flat_values, preferred_element_type=jnp.float32
    )
    probs_float = attn_probs.astype(jnp.float32)
    row_dot = jnp.sum(probs_float * prob_grad, -1, keepdims=True)
    score_grad = (probs_float * (prob_grad - row_dot) * HEAD ** (-0.5)).astype(jnp.bfloat16)
    d_query = jnp.einsum(
        "ghqm,gmhd->gqhd", score_grad, flat_keys, preferred_element_type=jnp.float32
    )
    d_query = d_query.astype(jnp.bfloat16).reshape(seq_dev, 1, local_cols)
    d_key = jnp.einsum("ghqm,gqhd->gmhd", score_grad, queries, preferred_element_type=jnp.float32)
    d_value = jnp.einsum(
        "ghqm,gqhd->gmhd", attn_probs, dout_blocks, preferred_element_type=jnp.float32
    )
    contrib = jnp.stack(
        [
            d_key.reshape(per_shard, NBR, BLOCK, heads_here, HEAD),
            d_value.reshape(per_shard, NBR, BLOCK, heads_here, HEAD),
        ],
        3,
    )
    ext_grad = (
        jnp.zeros((3 * per_shard, BLOCK, 2, heads_here, HEAD), jnp.float32)
        .at[ext_index]
        .add(contrib)
    )
    middle = ext_grad[per_shard : 2 * per_shard]
    from_right = from_behind(ext_grad[:per_shard].astype(jnp.bfloat16), "ctx", -1).astype(
        jnp.float32
    )
    from_left = from_behind(ext_grad[2 * per_shard :].astype(jnp.bfloat16), "ctx", 1).astype(
        jnp.float32
    )
    kv_grad = middle + from_right + from_left
    kv_rows = kv_grad.astype(jnp.bfloat16).reshape(seq_dev, 2, local_cols)
    d_project = jnp.concatenate([d_query, kv_rows], 1).reshape(seq_dev, 3 * local_cols)
    qkv_part = lax.dot_general(
        hidden, d_project, (((0,), (0,)), ((), ())), preferred_element_type=jnp.float32
    ).reshape(model_dim, 3, local_cols)
    hidden_part = as_rounded(
        lax.dot_general(
            d_project, flat_weight, (((1,), (1,)), ((), ())), preferred_element_type=jnp.float32
        )
    )
    d_hidden = lax.psum(hidden_part.astype(jnp.bfloat16), "src").astype(jnp.float32)
    d_normed = d_hidden * norm_gain
    d_start = upstream.astype(jnp.float32) + inv_std * (
        d_normed
        - jnp.mean(d_normed, -1, keepdims=True)
        - normed * jnp.mean(d_normed * normed, -1, keepdims=True)
    )
    d_start = d_start.astype(jnp.bfloat16)
    gain_part = jnp.sum(d_hidden * normed, 0)
    qkv_grad, out_grad, gain_grad = (
        lax.psum(qkv_part.astype(jnp.bfloat16), "ctx").astype(jnp.float32),
        lax.psum(out_part.astype(jnp.bfloat16), "ctx").astype(jnp.float32),
        lax.psum(gain_part.astype(jnp.bfloat16), "ctx").astype(jnp.float32),
    )
    got_grad = jnp.where(is_valid[:, None], d_start[jnp.clip(got_pos, 0, seq_dev - 1)], 0)
    row_share = lax.psum_scatter(
        lax.dot_general(
            got_rows, got_grad, (((0,), (0,)), ((), ())), preferred_element_type=jnp.float32
        ).astype(jnp.bfloat16),
        "ctx",
        scatter_dimension=0,
        tiled=True,
    )
    in_grad = lax.psum_scatter(row_share, "src", scatter_dimension=1, tiled=True).astype(
        jnp.float32
    )
    return (encoded, in_grad, gain_grad, qkv_grad, out_grad)


def solution(mesh):
    return jax.shard_map(
        local,
        mesh=mesh,
        in_specs=(
            P(("src", "ctx"), None),
            P(("src", "ctx")),
            P(),
            P(),
            P(None, None, "src"),
            P("src", None),
            P(),
            P("ctx", None),
        ),
        out_specs=(P("ctx", None), P("ctx", "src"), P(), P(None, None, "src"), P("src", None)),
        check_vma=False,
    )
```

profile of v0, /device:TPU:0, one launch (start us, length us, event | category | flops | bytes accessed | tf_op | source)
XLA Modules:
  0.0 899.4 jit_solution(9874884597815849275)
XLA Ops:
  8.0 2.3 reduce-window.6
  11.6 4.9 scatter_custom_fusion
  16.4 5.2 all-to-all-start
  21.6 8.4 scatter_custom_fusion.1
  30.0 4.5 all-to-all-start.1
  35.1 37.2 %all-to-all-done.1 = bf16[8,128,1536]{2,1,0:T(8,128)(2,1)} async-done(((bf16[8,128,1536]{2,1,0:T(8,128)(2,1)}), bf16[8,128,1536]{2,1,0:T(8,128)(2,1)}, u32[]{:S(2)}, u32[]{:S(2)}) %all-to-all-start.1) | async-done | bytes 3145760 | tf_op jit(solution)/shard_map/all_to_all | solution.py:72
  72.3 5.6 convolution_convert_fusion.4
  78.0 8.6 scatter_custom_fusion.2
  86.6 4.8 convert_element_type.115
  91.9 120.1 %all-reduce.6.cloned.1.call-done = bf16[2048,768]{1,0:T(8,128)(2,1)} async-done(((bf16[2048,768]{1,0:T(8,128)(2,1)}), bf16[2048,768]{1,0:T(8,128)(2,1)}) %all-reduce.6.cloned.1.call-update) | async-done | bytes 3145744 | tf_op jit(solution)/shard_map/psum | solution.py:80
  212.0 2.5 convert_reduce_fusion
  216.0 2.6 convolution_convert_fusion.2
  218.7 1.3 copy-done.9
  220.0 1.3 collective-permute-start.1
  221.3 4.2 collective-permute-start
  225.8 3.1 fusion.41
  230.4 2.1 pad_maximum_fusion.1
  232.5 1.3 copy.69
  233.8 3.5 copy.47
  237.3 6.3 gather_fusion
  243.6 6.3 fusion.70
  249.9 6.0 copy.48
  256.0 5.8 reshape_squeeze.9
  261.8 8.0 copy.54
  269.8 7.2 fusion.72
  277.1 17.6 %copy.51 = f32[16,4,128,512]{3,2,1,0:T(8,128)} copy(f32[16,4,128,512]{2,3,1,0:T(8,128)} %bitcast.137) | data formatting | bytes 33554432 | tf_op jit(solution)/shard_map/mul | solution.py:44
  294.7 9.9 %exponential_reduce_fusion = f32[16,4,128]{2,1,0:T(4,128)S(1)} fusion(f32[16,4,128,4,128]{2,4,3,1,0:T(8,128)} %get-tuple-element.24, f32[16,4,128]{2,1,0:T(4,128)S(1)} %get-tuple-element.23), kind=kLoop, calls=%fused_computation.12 | loop fusion | flops 8380416 | bytes 16842752 | tf_op jit(solution)/shard_map/reduce_sum | solution.py:47
  304.6 7.9 divide_convert_fusion
  312.5 8.2 fusion.52
  320.7 3.8 convolution_bitcast_fusion
  324.5 7.6 stack_reshape.7
  332.1 21.3 %fusion.29 = f32[16,512,4,48]{1,3,2,0:T(8,128)} fusion(bf16[16,4,128,512]{3,2,1,0:T(8,128)(2,1)} %copy-done.2, f32[16,4,128,512]{3,2,1,0:T(8,128)} %fusion.52, bf16[16,128,4,48]{1,0,3,2:T(8,128)(2,1)S(1)} %bitcast.147), kind=kOutput, calls=%fused_computation.53 | convolution fusion | flops 432022016 | bytes 32243712 | tf_op jit(solution)/shard_map/ghqm,gqhd->gmhd/dot_general | solution.py:127
  353.4 7.6 stack_reshape.6
  361.0 12.9 %pad_maximum_fusion = f32[16,4,128,2,4,48]{2,1,5,4,0,3:T(4,128)} fusion(f32[16,4,128,1,4,48]{2,1,5,4,0,3:T(4,128)} %stack_reshape.7, f32[16,4,128,1,4,48]{2,1,5,4,0,3:T(4,128)} %stack_reshape.6), kind=kLoop, calls=%fused_computation.13 | loop fusion | flops 3145728 | bytes 25165824 | tf_op jit(solution)/shard_map/stack | solution.py:131
  373.9 10.9 %copy.59 = f32[16,4,128,2,4,48]{2,5,4,3,1,0:T(8,128)} copy(f32[16,4,128,2,4,48]{2,1,5,4,0,3:T(4,128)} %pad_maximum_fusion) | data formatting | bytes 25165824 | tf_op jit(solution)/shard_map/stack | solution.py:131
  384.8 4.8 broadcast_in_dim.58
  389.6 31.6 %scatter_fusion = f32[48,128,2,4,48]{1,4,3,2,0:T(8,128)} fusion(f32[48,128,2,4,48]{1,4,3,2,0:T(8,128)} %broadcast_in_dim.58, s32[64]{0:T(128)S(1)} %reshape.161, f32[64,128,2,4,48]{1,4,3,2,0:T(8,128)} %bitcast.136), kind=kCustom, calls=%fused_computation.5 | custom fusion | flops 3145728 | bytes 37748992 | tf_op jit(solution)/shard_map/scatter-add | solution.py:141
  421.2 4.8 convert.4
  426.0 2.3 fusion.71
  428.3 27.6 %collective-permute-start.3 = (bf16[16,128,2,4,48]{1,4,3,2,0:T(8,128)(2,1)}, bf16[16,128,2,4,48]{1,4,3,2,0:T(8,128)(2,1)}, u32[]{:S(2)}, u32[]{:S(2)}) collective-permute-start(bf16[16,128,2,4,48]{1,4,3,2,0:T(8,128)(2,1)} %get-tuple-element.15), channel_id=1, source_target_pairs={{0,1},{1,2},{2,3},{3,4},{4,5},{5,6},{6,7},{8,9},{9,10},{10,11},{11... | collective-permute-start | bytes 4718600 | tf_op jit(solution)/shard_map/ppermute | solution.py:34
  455.9 1.7 collective-permute-start.2
  457.6 6.4 fusion.42
  464.6 2.7 convolution_convert_fusion.1
  467.3 5.7 reshape_squeeze.11
  473.0 21.3 %fusion.43 = bf16[16,128,4,48]{1,3,2,0:T(8,128)(2,1)S(1)} fusion(bf16[16,512,4,48]{1,3,2,0:T(8,128)(2,1)} %reshape_squeeze.11, bf16[16,4,128,512]{3,2,1,0:T(8,128)(2,1)} %copy-done.2, f32[16,4,128,512]{3,2,1,0:T(8,128)} %fusion.52), kind=kOutput, calls=%fused_computation.67 | convolution fusion | flops 432415232 | bytes 29097984 | tf_op jit(solution)/shard_map/ghqm,gmhd->gqhd/dot_general | solution.py:123
  496.1 3.5 fusion.23
  499.7 2.2 copy.60
  501.8 2.5 reshape.157
  504.4 1.3 constant_dynamic-update-slice_fusion
  505.7 6.0 bitcast_convert_fusion
  512.4 227.1 %all-reduce.10.cloned.1.call-done = (bf16[2048,768]{1,0:T(8,128)(2,1)}, bf16[2048,768]{1,0:T(8,128)(2,1)}) async-done(((bf16[2048,768]{1,0:T(8,128)(2,1)}, bf16[2048,768]{1,0:T(8,128)(2,1)}), (bf16[2048,768]{1,0:T(8,128)(2,1)}, bf16[2048,768]{1,0:T(8,128)(2,1)})) %all-reduce.10.cloned.1.call-update) | async-done | bytes 6291472 | tf_op jit(solution)/shard_map/psum | solution.py:108
  739.5 5.8 fusion.20
  745.4 7.9 fusion.17
  753.4 6.8 gather_fusion.1
  760.1 6.1 convolution_convert_fusion
  766.3 3.4 convolution_convert_fusion.6
  769.7 6.2 fusion.35
  776.0 31.9 %reduce-scatter.5.cloned.1.call-done = bf16[192,768]{1,0:T(8,128)(2,1)} async-done(((bf16[1536,768]{1,0:T(8,128)(2,1)}), bf16[192,768]{1,0:T(8,128)(2,1)}) %reduce-scatter.5.cloned.1.call-update) | async-done | bytes 294928 | tf_op jit(solution)/shard_map/reduce_scatter | solution.py:176
  807.8 1.9 copy.64
  809.7 59.4 %all-reduce.8.cloned.1.call-done = (bf16[768,3,192]{0,2,1:T(8,128)(2,1)}, bf16[192,768]{1,0:T(8,128)(2,1)}) async-done(((bf16[768,3,192]{0,2,1:T(8,128)(2,1)}, bf16[192,768]{1,0:T(8,128)(2,1)}), (bf16[768,3,192]{0,2,1:T(8,128)(2,1)}, bf16[192,768]{1,0:T(8,128)(2,1)})) %all-reduce.8.cloned.1.call-update) | async-done | bytes 1179664 | tf_op jit(solution)/shard_map/psum | solution.py:171
  869.1 2.5 convert_element_type.142
  871.7 1.8 convert_element_type.144
  873.5 12.2 %psum.45 = bf16[768]{0:T(1024)(128)(2,1)S(1)} all-reduce(bf16[768]{0:T(1024)(128)(2,1)S(1)} %get-tuple-element.5), channel_id=1, replica_groups=mesh['src'=4,'ctx'=8] {'ctx'}, use_global_device_ids=true, to_apply=%region_20.21 | all-reduce | flops 768 | bytes 3072 | tf_op jit(solution)/shard_map/psum | solution.py:173
  886.3 4.7 reduce-scatter.7.cloned.1.call-done
  (89 shorter events, 12.0 us)
Async XLA Ops:
  7.2 65.2 %copy-start = (bf16[1536,768]{1,0:T(8,128)(2,1)S(1)}, bf16[1536,768]{1,0:T(8,128)(2,1)}, u32[]{:S(2)}) copy-start(bf16[1536,768]{1,0:T(8,128)(2,1)} %param.10) | copy-start | bytes 7077892
  16.4 13.5 %all-to-all-start = ((s32[8,1,128]{2,1,0:T(1,128)}), s32[8,1,128]{2,1,0:T(1,128)S(1)}, u32[]{:S(2)}, u32[]{:S(2)}) async-start(s32[8,1,128]{2,1,0:T(1,128)} %bitcast.2), calls=%async_computation | async-start | bytes 8192 | tf_op jit(solution)/shard_map/all_to_all | solution.py:69
  30.0 48.0 %copy-start.15 = (s32[8,1,128]{2,1,0:T(1,128)}, s32[8,1,128]{2,1,0:T(1,128)S(1)}, u32[]{:S(2)}) copy-start(s32[8,1,128]{2,1,0:T(1,128)S(1)} %all-to-all-done) | copy-start | bytes 12292
  30.0 42.3 %all-to-all-start.1 = ((bf16[8,128,1536]{2,1,0:T(8,128)(2,1)}), bf16[8,128,1536]{2,1,0:T(8,128)(2,1)}, u32[]{:S(2)}, u32[]{:S(2)}) async-start(bf16[8,128,1536]{2,1,0:T(8,128)(2,1)} %bitcast.143), calls=%async_computation.1 | async-start | bytes 6291456 | tf_op jit(solution)/shard_map/all_to_all | solution.py:72
  34.5 177.5 %all-reduce.6.cloned.1.call-start = ((), (), s32[]{:S(2)}) async-start(), calls=%async_computation.4 | async-start | bytes 6291456 | tf_op jit(solution)/shard_map/psum | solution.py:80
  91.3 124.6 %copy-start.18 = (f32[768]{0:T(1024)S(1)}, f32[768]{0:T(1024)}, u32[]{:S(2)}) copy-start(f32[768]{0:T(1024)} %param.11) | copy-start | bytes 9220
  91.3 124.6 %copy-start.21 = (bf16[768,3,192]{0,2,1:T(8,128)(2,1)S(1)}, bf16[768,3,192]{0,2,1:T(8,128)(2,1)}, u32[]{:S(2)}) copy-start(bf16[768,3,192]{0,2,1:T(8,128)(2,1)} %param.12) | copy-start | bytes 2654212
  91.4 648.2 %all-reduce.10.cloned.1.call-start = ((), (), s32[]{:S(2)}) async-start(), calls=%async_computation.8 | async-start | bytes 12582912 | tf_op jit(solution)/shard_map/psum | solution.py:108
  212.0 2.8 copy-start.3
  214.8 3.8 copy-start.11
  215.9 2.7 copy-start.13
  215.9 9.6 %copy-start.20 = (s32[128,4]{0,1:T(4,128)S(1)}, s32[128,4]{0,1:T(4,128)}, u32[]{:S(2)}) copy-start(s32[128,4]{0,1:T(4,128)} %param.14) | copy-start | bytes 6148
  216.0 9.8 %copy-start.10 = (bf16[192,768]{1,0:T(8,128)(2,1)S(1)}, bf16[192,768]{1,0:T(8,128)(2,1)}, u32[]{:S(2)}) copy-start(bf16[192,768]{1,0:T(8,128)(2,1)} %param.13) | copy-start | bytes 884740
  218.6 1.4 copy-start.9
  220.0 10.4 %collective-permute-start.1 = (bf16[2048,2,192]{0,2,1:T(8,128)(2,1)S(1)}, bf16[2048,2,192]{0,2,1:T(8,128)(2,1)}, u32[]{:S(2)}, u32[]{:S(2)}) collective-permute-start(bf16[2048,2,192]{0,2,1:T(8,128)(2,1)S(1)} %slice.43), channel_id=1, source_target_pairs={{1,0},{2,1},{3,2},{4,3},{5,4},{6,5},{7,6},{9,8},{10,9},{11,10},{12... | collective-permute-start | bytes 4718600 | tf_op jit(solution)/shard_map/ppermute | solution.py:24
  221.3 9.1 %collective-permute-start = (bf16[2048,2,192]{0,2,1:T(8,128)(2,1)S(1)}, bf16[2048,2,192]{0,2,1:T(8,128)(2,1)}, u32[]{:S(2)}, u32[]{:S(2)}) collective-permute-start(bf16[2048,2,192]{0,2,1:T(8,128)(2,1)S(1)} %slice.43), channel_id=1, source_target_pairs={{0,1},{1,2},{2,3},{3,4},{4,5},{5,6},{6,7},{8,9},{9,10},{10,11},{11... | collective-permute-start | bytes 4718600 | tf_op jit(solution)/shard_map/ppermute | solution.py:22
  261.8 8.0 copy-start.6
  304.6 7.9 copy-start.4
  312.5 8.2 copy-start.2
  426.0 31.6 %copy-start.5 = (bf16[16,512,4,48]{1,3,2,0:T(8,128)(2,1)S(1)}, bf16[16,512,4,48]{1,3,2,0:T(8,128)(2,1)}, u32[]{:S(2)}) copy-start(bf16[16,512,4,48]{1,3,2,0:T(8,128)(2,1)} %reshape_squeeze.9) | copy-start | bytes 9437188
  428.3 67.9 %collective-permute-start.3 = (bf16[16,128,2,4,48]{1,4,3,2,0:T(8,128)(2,1)}, bf16[16,128,2,4,48]{1,4,3,2,0:T(8,128)(2,1)}, u32[]{:S(2)}, u32[]{:S(2)}) collective-permute-start(bf16[16,128,2,4,48]{1,4,3,2,0:T(8,128)(2,1)} %get-tuple-element.15), channel_id=1, source_target_pairs={{0,1},{1,2},{2,3},{3,4},{4,5},{5,6},{6,7},{8,9},{9,10},{10,11},{11... | collective-permute-start | bytes 4718600 | tf_op jit(solution)/shard_map/ppermute | solution.py:34
  455.9 40.2 %collective-permute-start.2 = (bf16[16,128,2,4,48]{1,4,3,2,0:T(8,128)(2,1)}, bf16[16,128,2,4,48]{1,4,3,2,0:T(8,128)(2,1)}, u32[]{:S(2)}, u32[]{:S(2)}) collective-permute-start(bf16[16,128,2,4,48]{1,4,3,2,0:T(8,128)(2,1)} %get-tuple-element.14), channel_id=1, source_target_pairs={{1,0},{2,1},{3,2},{4,3},{5,4},{6,5},{7,6},{9,8},{10,9},{11,10},{12... | collective-permute-start | bytes 4718600 | tf_op jit(solution)/shard_map/ppermute | solution.py:34
  499.7 6.1 copy-start.22
  511.7 0.7 copy-start.16
  511.8 0.7 copy-start.17
  511.8 227.8 %copy-start.12 = (f32[2048]{0:T(1024)S(1)}, f32[2048]{0:T(1024)}, u32[]{:S(2)}) copy-start(f32[2048]{0:T(1024)} %copy-done.11) | copy-start | bytes 24580
  511.8 227.8 %copy-start.14 = (f32[2048]{0:T(1024)S(1)}, f32[2048]{0:T(1024)}, u32[]{:S(2)}) copy-start(f32[2048]{0:T(1024)} %copy-done.13) | copy-start | bytes 24580
  511.8 227.8 %copy-start.19 = (f32[768]{0:T(1024)S(1)}, f32[768]{0:T(1024)}, u32[]{:S(2)}) copy-start(f32[768]{0:T(1024)} %param.11) | copy-start | bytes 9220
  511.8 296.0 %reduce-scatter.5.cloned.1.call-start = ((), (), s32[]{:S(2)}) async-start(), calls=%async_computation.5 | async-start | bytes 2654208 | tf_op jit(solution)/shard_map/reduce_scatter | solution.py:176
  739.5 5.9 copy-start.7
  739.5 5.9 copy-start.8
  766.2 102.9 %all-reduce.8.cloned.1.call-start = ((), (), s32[]{:S(2)}) async-start(), calls=%async_computation.7 | async-start | bytes 2359296 | tf_op jit(solution)/shard_map/psum | solution.py:171
  769.7 123.0 %copy-start.1 = (bf16[1536,768]{1,0:T(8,128)(2,1)S(1)}, bf16[1536,768]{1,0:T(8,128)(2,1)}, u32[]{:S(2)}) copy-start(bf16[1536,768]{1,0:T(8,128)(2,1)} %param.10) | copy-start | bytes 7077892
  775.9 115.0 %reduce-scatter.7.cloned.1.call-start = ((), (), s32[]{:S(2)}) async-start(), calls=%async_computation.6 | async-start | bytes 491520
Sparse Core Ops, SparseCore 0:
  91.5 120.4 all-reduce.5
  511.9 227.5 all-reduce.9
  766.4 41.4 reduce-scatter.4
  811.8 57.2 all-reduce.7
  871.3 19.6 reduce-scatter.6
where the time goes:
time: 909 us; the launch traced here: 899 us
  waiting for transfers between devices  480 us (53%)
  local copies, waits for them, and re-layouts  129 us (14%)
  other arithmetic  114 us (13%)
  matrix products  104 us (11%)
  starting transfers between devices  45.3 us (5%)
  between operations  14.4 us (2%)
  blocking collectives  12.2 us (1%)
    psum x1, waiting for transfers between devices, local(): lax.psum(partial_out.astype(jnp.bfloat16), 'src').astype(jnp.float32)  227 us
    psum x1, waiting for transfers between devices, local(): start_x = lax.psum(placed.astype(jnp.bfloat16), 'src')  120 us
    psum x1, waiting for transfers between devices, local(): lax.psum(qkv_part.astype(jnp.bfloat16), 'ctx').astype(jnp.float32)  59.4 us
    all_to_all x1, waiting for transfers between devices, local(): lax.all_to_all(send_rows.reshape(shards, capacity, -1), 'ctx', split_axis...  37.2 us
    reduce_scatter x1, waiting for transfers between devices, local(): lax.psum_scatter(lax.dot_general(got_rows, got_grad, (((0,), (0,)), ((),...  31.9 us
    scatter-add x1, other arithmetic, local(): ext_grad = jnp.zeros((3 * per_shard, BLOCK, 2, heads_here, HEAD), jnp.flo...  31.6 us
    ppermute x2, starting transfers between devices, from_behind(): lax.ppermute(value, axis, [(source, source + steps) for source in range(i...  29.3 us
    another operation x3, local copies, waits for them, and re-layouts, local(): jnp.stack([d_key.reshape(per_shard, NBR, BLOCK, heads_here, HEAD), d_valu...  26 us
  transfers between devices with their start and end apart: 11, of which 6 were waited for; matrix products, arithmetic and copies ran while one was open for 8% of the time, Pallas kernels for 0%

commit v1 on v0

v1 whole, which is shorter than its diff:
```python
import functools

import jax
import jax.numpy as jnp
from jax import lax
from jax.experimental import pallas as pl
from jax.experimental.pallas import tpu as pltpu
from jax.sharding import PartitionSpec as P

HEAD = 48
BLOCK = 128
NBR = 4
EPS = 1e-05
SCALE = HEAD ** (-0.5)
F32 = jnp.float32
BF16 = jnp.bfloat16
VMEM_BYTES = 52 * 1024 * 1024


def dot(a, b, ca, cb):
    return lax.dot_general(a, b, (((ca,), (cb,)), ((), ())), preferred_element_type=F32)


def params():
    return pltpu.CompilerParams(
        vmem_limit_bytes=VMEM_BYTES, dimension_semantics=("arbitrary",)
    )


def cost(flops, bytes_accessed, exps=0):
    return pl.CostEstimate(flops=flops, bytes_accessed=bytes_accessed, transcendentals=exps)


def centre(x):
    centred = x - jnp.mean(x, -1, keepdims=True)
    inv_std = lax.rsqrt(jnp.mean(centred * centred, -1, keepdims=True) + EPS)
    return centred * inv_std, inv_std


def project_kernel(x_ref, gain_ref, wt_ref, hidden_ref, q_ref, kv_ref):
    normed, _ = centre(x_ref[...].astype(F32))
    hidden = (normed * gain_ref[...]).astype(BF16)
    hidden_ref[...] = hidden
    cols = q_ref.shape[1]
    out = dot(wt_ref[...], hidden, 1, 1).astype(BF16)
    for g in range(q_ref.shape[0]):
        lanes = slice(g * BLOCK, (g + 1) * BLOCK)
        q_ref[g] = out[:cols, lanes]
        kv_ref[g] = out[cols:, lanes]


def project_rows(x, gain, wt, cols):
    rows, width = x.shape
    step = 4
    blocks = rows // BLOCK
    return pl.pallas_call(
        project_kernel,
        grid=(blocks // step,),
        in_specs=[
            pl.BlockSpec((step * BLOCK, width), lambda i: (i, 0)),
            pl.BlockSpec((1, width), lambda i: (0, 0)),
            pl.BlockSpec(wt.shape, lambda i: (0, 0)),
        ],
        out_specs=[
            pl.BlockSpec((step * BLOCK, width), lambda i: (i, 0)),
            pl.BlockSpec((step, cols, BLOCK), lambda i: (i, 0, 0)),
            pl.BlockSpec((step, 2 * cols, BLOCK), lambda i: (i, 0, 0)),
        ],
        out_shape=[
            jax.ShapeDtypeStruct((rows, width), BF16),
            jax.ShapeDtypeStruct((blocks, cols, BLOCK), BF16),
            jax.ShapeDtypeStruct((blocks, 2 * cols, BLOCK), BF16),
        ],
        compiler_params=params(),
        cost_estimate=cost(2 * rows * width * 3 * cols, 4 * rows * width + 8 * rows * cols),
    )(x, gain, wt)


def neighbour_rows(index_ref, kv_ref, low, high):
    b = pl.program_id(0)
    return jnp.concatenate(
        [kv_ref[index_ref[b * NBR + j], low:high, :] for j in range(NBR)], axis=1
    )


def forward_kernel(index_ref, q_ref, kv_ref, ow_ref, up_ref, part_ref, probs_ref, og_ref):
    cols = q_ref.shape[1]
    mixed = []
    for h in range(cols // HEAD):
        low, high = h * HEAD, (h + 1) * HEAD
        keys = neighbour_rows(index_ref, kv_ref, low, high)
        values = neighbour_rows(index_ref, kv_ref, cols + low, cols + high)
        scores = dot(q_ref[0, low:high, :], keys, 0, 0) * SCALE
        powers = jnp.exp(scores - jnp.max(scores, -1, keepdims=True))
        inverse = 1.0 / jnp.sum(powers, -1, keepdims=True)
        probs = (powers * inverse).astype(BF16)
        probs_ref[0, h] = probs
        mixed.append(dot(values, probs, 1, 1).astype(BF16))
    mixed = jnp.concatenate(mixed, axis=0)
    part_ref[...] = dot(mixed, ow_ref[...], 0, 0).astype(BF16)

    @pl.when(pl.program_id(0) == 0)
    def _():
        og_ref[...] = jnp.zeros_like(og_ref)

    og_ref[...] += dot(mixed, up_ref[...], 1, 0)


def attend_forward(index, q, kv, ow, up):
    blocks, cols, _ = q.shape
    rows, width = up.shape
    heads = cols // HEAD
    whole = lambda s: pl.BlockSpec(s, lambda i, r: (0,) * len(s))
    return pl.pallas_call(
        forward_kernel,
        grid_spec=pltpu.PrefetchScalarGridSpec(
            num_scalar_prefetch=1,
            grid=(blocks,),
            in_specs=[
                pl.BlockSpec((1, cols, BLOCK), lambda i, r: (i, 0, 0)),
                whole(kv.shape),
                whole(ow.shape),
                pl.BlockSpec((BLOCK, width), lambda i, r: (i, 0)),
            ],
            out_specs=[
                pl.BlockSpec((BLOCK, width), lambda i, r: (i, 0)),
                pl.BlockSpec((1, heads, BLOCK, NBR * BLOCK), lambda i, r: (i, 0, 0, 0)),
                whole(ow.shape),
            ],
        ),
        out_shape=[
            jax.ShapeDtypeStruct((rows, width), BF16),
            jax.ShapeDtypeStruct((blocks, heads, BLOCK, NBR * BLOCK), BF16),
            jax.ShapeDtypeStruct(ow.shape, F32),
        ],
        compiler_params=params(),
        cost_estimate=cost(
            16 * rows * cols * NBR * BLOCK, 40 * rows * width, rows * heads * NBR * BLOCK
        ),
    )(index, q, kv, ow, up)


def backward_kernel(
    index_ref, q_ref, kv_ref, ow_ref, up_ref, probs_ref,
    dq_ref, before_ref, own_ref, after_ref, total_ref,
):
    b = pl.program_id(0)
    cols = q_ref.shape[1]
    per_shard = own_ref.shape[0]

    @pl.when(b == 0)
    def _():
        @pl.loop(0, 3 * per_shard)
        def _(i):
            total_ref[i] = jnp.zeros(total_ref.shape[1:], F32)

    d_mixed = dot(ow_ref[...], up_ref[...], 1, 1).astype(BF16)
    key_terms, value_terms = [], []
    for h in range(cols // HEAD):
        low, high = h * HEAD, (h + 1) * HEAD
        keys = neighbour_rows(index_ref, kv_ref, low, high)
        values = neighbour_rows(index_ref, kv_ref, cols + low, cols + high)
        probs = probs_ref[0, h]
        d_out = d_mixed[low:high, :]
        prob_grad = dot(d_out, values, 0, 0)
        weight = probs.astype(F32)
        row_dot = jnp.sum(weight * prob_grad, -1, keepdims=True)
        score_grad = (weight * (prob_grad - row_dot) * SCALE).astype(BF16)
        dq_ref[0, low:high, :] = dot(keys, score_grad, 1, 1).astype(BF16)
        key_terms.append(dot(q_ref[0, low:high, :], score_grad, 1, 0))
        value_terms.append(dot(d_out, probs, 1, 0))
    terms = jnp.concatenate(key_terms + value_terms, axis=0)
    for j in range(NBR):
        total_ref[index_ref[b * NBR + j]] += terms[:, j * BLOCK : (j + 1) * BLOCK]

    @pl.when(b == per_shard - 1)
    def _():
        @pl.loop(0, per_shard)
        def _(i):
            before_ref[i] = total_ref[i].astype(BF16)
            own_ref[i] = total_ref[per_shard + i]
            after_ref[i] = total_ref[2 * per_shard + i].astype(BF16)


def attend_backward(index, q, kv, ow, up, probs):
    blocks, cols, _ = q.shape
    rows, width = up.shape
    heads = cols // HEAD
    whole = lambda s: pl.BlockSpec(s, lambda i, r: (0,) * len(s))
    grads = (blocks, 2 * cols, BLOCK)
    return pl.pallas_call(
        backward_kernel,
        grid_spec=pltpu.PrefetchScalarGridSpec(
            num_scalar_prefetch=1,
            grid=(blocks,),
            in_specs=[
                pl.BlockSpec((1, cols, BLOCK), lambda i, r: (i, 0, 0)),
                whole(kv.shape),
                whole(ow.shape),
                pl.BlockSpec((BLOCK, width), lambda i, r: (i, 0)),
                pl.BlockSpec((1, heads, BLOCK, NBR * BLOCK), lambda i, r: (i, 0, 0, 0)),
            ],
            out_specs=[
                pl.BlockSpec((1, cols, BLOCK), lambda i, r: (i, 0, 0)),
                whole(grads),
                whole(grads),
                whole(grads),
            ],
            scratch_shapes=[pltpu.VMEM((3 * blocks, 2 * cols, BLOCK), F32)],
        ),
        out_shape=[
            jax.ShapeDtypeStruct(q.shape, BF16),
            jax.ShapeDtypeStruct(grads, BF16),
            jax.ShapeDtypeStruct(grads, F32),
            jax.ShapeDtypeStruct(grads, BF16),
        ],
        compiler_params=params(),
        cost_estimate=cost(32 * rows * cols * NBR * BLOCK, 60 * rows * width),
    )(index, q, kv, ow, up, probs)


def product_kernel(dq_ref, own_ref, right_ref, left_ref, hid_ref, wt_ref, part_ref, qg_ref, dp_ref):
    i = pl.program_id(0)
    cols = dq_ref.shape[1]
    for g in range(dq_ref.shape[0]):
        lanes = slice(g * BLOCK, (g + 1) * BLOCK)
        dp_ref[:cols, lanes] = dq_ref[g]
        total = own_ref[g] + right_ref[g].astype(F32) + left_ref[g].astype(F32)
        dp_ref[cols:, lanes] = total.astype(BF16)
    dp = dp_ref[...]
    part_ref[...] = dot(dp, wt_ref[...], 0, 0).astype(BF16)

    @pl.when(i == 0)
    def _():
        qg_ref[...] = jnp.zeros_like(qg_ref)

    qg_ref[...] += dot(dp, hid_ref[...], 1, 0)


def gradient_products(dq, own, right, left, hidden, wt):
    blocks, cols, _ = dq.shape
    rows, width = hidden.shape
    step = 4
    side = pl.BlockSpec((step, 2 * cols, BLOCK), lambda i: (i, 0, 0))
    return pl.pallas_call(
        product_kernel,
        grid=(blocks // step,),
        in_specs=[
            pl.BlockSpec((step, cols, BLOCK), lambda i: (i, 0, 0)),
            side,
            side,
            side,
            pl.BlockSpec((step * BLOCK, width), lambda i: (i, 0)),
            pl.BlockSpec(wt.shape, lambda i: (0, 0)),
        ],
        out_specs=[
            pl.BlockSpec((step * BLOCK, width), lambda i: (i, 0)),
            pl.BlockSpec(wt.shape, lambda i: (0, 0)),
        ],
        out_shape=[
            jax.ShapeDtypeStruct((rows, width), BF16),
            jax.ShapeDtypeStruct(wt.shape, F32),
        ],
        scratch_shapes=[pltpu.VMEM((3 * cols, step * BLOCK), BF16)],
        compiler_params=params(),
        cost_estimate=cost(4 * rows * width * 3 * cols, 4 * rows * width + 18 * rows * cols),
    )(dq, own, right, left, hidden, wt)


def norm_back_kernel(dh_ref, x_ref, up_ref, gain_ref, ds_ref, gg_ref):
    normed, inv_std = centre(x_ref[...].astype(F32))
    d_hidden = dh_ref[...].astype(F32)
    grad = d_hidden * gain_ref[...]
    d_start = up_ref[...].astype(F32) + inv_std * (
        grad
        - jnp.mean(grad, -1, keepdims=True)
        - normed * jnp.mean(grad * normed, -1, keepdims=True)
    )
    ds_ref[...] = d_start.astype(BF16)

    @pl.when(pl.program_id(0) == 0)
    def _():
        gg_ref[...] = jnp.zeros_like(gg_ref)

    gg_ref[...] += jnp.sum(d_hidden * normed, 0, keepdims=True)


def norm_back(d_hidden, x, up, gain):
    rows, width = x.shape
    step = 4 * BLOCK
    tile = pl.BlockSpec((step, width), lambda i: (i, 0))
    line = pl.BlockSpec((1, width), lambda i: (0, 0))
    return pl.pallas_call(
        norm_back_kernel,
        grid=(rows // step,),
        in_specs=[tile, tile, tile, line],
        out_specs=[tile, line],
        out_shape=[
            jax.ShapeDtypeStruct((rows, width), BF16),
            jax.ShapeDtypeStruct((1, width), F32),
        ],
        compiler_params=params(),
        cost_estimate=cost(30 * rows * width, 8 * rows * width),
    )(d_hidden, x, up, gain)


def from_behind(value, axis, steps):
    count = lax.axis_size(axis)
    initial, last = (max(0, -steps), min(count, count - steps))
    return lax.ppermute(value, axis, [(source, source + steps) for source in range(initial, last)])


def mm(a, b):
    return jnp.dot(a, b, preferred_element_type=F32).astype(BF16)


def local(embeddings, positions, in_weight, norm_gain, qkv_weight, out_weight, neighbors, upstream):
    shards = lax.axis_size("ctx")
    my_shard = lax.axis_index("ctx")
    seq_dev, model_dim = upstream.shape
    per_shard = seq_dev // BLOCK
    produced = positions.shape[0]
    capacity = produced // shards
    cols = qkv_weight.shape[2]
    wt = qkv_weight.reshape(model_dim, 3 * cols).T
    gain = norm_gain.reshape(1, model_dim)

    target = jnp.floor_divide(positions, seq_dev)
    onehot = (target[:, None] == jnp.arange(shards, dtype=jnp.int32)[None, :]).astype(jnp.int32)
    order_in = jnp.sum((jnp.cumsum(onehot, 0) - onehot) * onehot, 1)
    slot_index = jnp.where(positions >= 0, target * capacity + order_in, produced)
    local_pos = positions - target * seq_dev
    slots = jnp.arange(produced, dtype=jnp.int32)
    in_slot = slots[:, None] == slot_index[None, :]
    send_pos = jnp.max(jnp.where(in_slot, local_pos[None, :], -1), 1)
    pick = in_slot.astype(BF16)
    send_proj = mm(pick, mm(embeddings, in_weight))
    swap = functools.partial(
        lax.all_to_all, axis_name="ctx", split_axis=0, concat_axis=0, tiled=True
    )
    got_pos = swap(send_pos.reshape(shards, capacity)).reshape(produced)
    got_proj = swap(send_proj.reshape(shards, capacity, -1)).reshape(produced, -1)
    send_rows, got_proj = lax.optimization_barrier((mm(pick, embeddings), got_proj))
    got_rows = swap(send_rows.reshape(shards, capacity, -1)).reshape(produced, -1)
    place = (got_pos[None, :] == jnp.arange(seq_dev, dtype=jnp.int32)[:, None]).astype(BF16)
    start_x = lax.psum(mm(place, got_proj), "src")
    slide = mm(place, got_rows)

    hidden, q, kv = project_rows(start_x, gain, wt, cols)
    ext_kv = jnp.concatenate(
        [from_behind(kv, "ctx", 1), kv, from_behind(kv, "ctx", -1)], axis=0
    )
    my_lists = lax.dynamic_slice_in_dim(neighbors, my_shard * per_shard, per_shard, 0)
    index = (my_lists - (my_shard - 1) * per_shard).reshape(-1)
    part, probs, out_part = attend_forward(index, q, ext_kv, out_weight, upstream)
    attn_total = lax.psum(part, "src")
    out_sum = lax.psum(out_part.astype(BF16), "ctx")
    dq, before, own, after = attend_backward(index, q, ext_kv, out_weight, upstream, probs)
    from_right = from_behind(before, "ctx", -1)
    from_left = from_behind(after, "ctx", 1)
    hidden_part, qkv_part = gradient_products(dq, own, from_right, from_left, hidden, wt)
    hidden_part, qkv_part, attn_total, out_sum = lax.optimization_barrier(
        (hidden_part, qkv_part, attn_total, out_sum)
    )
    encoded = (start_x.astype(F32) + attn_total.astype(F32)).astype(BF16)
    d_hidden = lax.psum(hidden_part, "src")
    qkv_sum = lax.psum(qkv_part.astype(BF16), "ctx")
    d_hidden, qkv_sum, slide = lax.optimization_barrier((d_hidden, qkv_sum, slide))
    d_start, gain_part = norm_back(d_hidden, start_x, upstream, gain)
    in_part = lax.dot_general(slide, d_start, (((0,), (0,)), ((), ())), preferred_element_type=F32)
    row_share = lax.psum_scatter(in_part.astype(BF16), "ctx", scatter_dimension=0, tiled=True)
    in_grad = lax.psum_scatter(row_share, "src", scatter_dimension=1, tiled=True)
    gain_sum = lax.psum(gain_part.astype(BF16), "ctx").reshape(model_dim)
    qkv_grad = qkv_sum.T.reshape(model_dim, 3, cols)
    return (
        encoded,
        in_grad.astype(F32),
        gain_sum.astype(F32),
        qkv_grad.astype(F32),
        out_sum.astype(F32),
    )


def solution(mesh):
    return jax.shard_map(
        local,
        mesh=mesh,
        in_specs=(
            P(("src", "ctx"), None),
            P(("src", "ctx")),
            P(),
            P(),
            P(None, None, "src"),
            P("src", None),
            P(),
            P("ctx", None),
        ),
        out_specs=(P("ctx", None), P("ctx", "src"), P(), P(None, None, "src"), P("src", None)),
        check_vma=False,
    )
```

time: 909 us -> 719 us (0.79); the launches traced: 899 us -> 719 us
  local copies, waits for them, and re-layouts: 129 us -> 9.57 us
  Pallas kernels: 0 us -> 99.5 us
  other arithmetic: 114 us -> 18.7 us
  matrix products: 104 us -> 37.1 us
    pallas_call x0 -> x5, Pallas kernels: none -> 99.5 us  [the longest x1 37.6 us: attend_forward(): pl.pallas_call(forward_kernel, grid_spec=pltpu.PrefetchScalarGridSpec(num...]
    dot_general x14 -> x5, matrix products: 104 us -> 37.1 us  [the longest x4 28.7 us: mm(): return jnp.dot(a, b, preferred_element_type=F32).astype(BF16)]
    another operation x5 -> x0, local copies, waits for them, and re-layouts: 37.5 us -> none  [the longest x3 26 us: local(): jnp.stack([d_key.reshape(per_shard, NBR, BLOCK, heads_here, HEAD), d_valu...]
    scatter-add x1 -> x0, other arithmetic: 31.6 us -> none  [local(): ext_grad = jnp.zeros((3 * per_shard, BLOCK, 2, heads_here, HEAD), jnp.flo...]
    slice x6 -> x1, local copies, waits for them, and re-layouts: 23 us -> 0.28 us  [the longest x2 14.4 us: local(): key_rows = chosen[:, :, :, 0]]
    reduce_sum x4 -> x0, other arithmetic: 19.3 us -> none  [the longest x1 9.86 us: attend_probs(): row_sum = jnp.sum(powers, -1, keepdims=True)]
    another operation x4 -> x2, other arithmetic: 20.1 us -> 2.43 us  [the longest x1 12.9 us: local(): jnp.stack([d_key.reshape(per_shard, NBR, BLOCK, heads_here, HEAD), d_valu...]
    mul x1 -> x0, local copies, waits for them, and re-layouts: 17.6 us -> none  [attend_probs(): scores.reshape(num_blocks, head_count, block_rows, -1) * HEAD ** (-0.5)]
  transfers between devices with their start and end apart: 11 -> 14, of which waited for: 6 -> 8; matrix products, arithmetic and copies ran while one was open for 8% -> 4% of each run, Pallas kernels for 0% -> 6%
where the time goes in v1:
time: 719 us
  waiting for transfers between devices  473 us (66%)
  Pallas kernels  99.5 us (14%)
  starting transfers between devices  53.5 us (7%)
  matrix products  37.1 us (5%)
  other arithmetic  18.7 us (3%)
  between operations  14.3 us (2%)
  blocking collectives  12.9 us (2%)
  local copies, waits for them, and re-layouts  9.57 us (1%)
    psum x1, waiting for transfers between devices, local(): start_x = lax.psum(mm(place, got_proj), 'src')  123 us
    psum x1, waiting for transfers between devices, local(): d_hidden = lax.psum(hidden_part, 'src')  123 us
    psum x1, waiting for transfers between devices, local(): attn_total = lax.psum(part, 'src')  119 us
    psum x1, waiting for transfers between devices, local(): qkv_sum = lax.psum(qkv_part.astype(BF16), 'ctx')  45 us
    reduce_scatter x1, waiting for transfers between devices, local(): lax.psum_scatter(in_part.astype(BF16), 'ctx', scatter_dimension=0, tiled=...  40.8 us
    ppermute x4, starting transfers between devices, from_behind(): lax.ppermute(value, axis, [(source, source + steps) for source in range(i...  40.1 us
    pallas_call x1, Pallas kernels, attend_forward(): pl.pallas_call(forward_kernel, grid_spec=pltpu.PrefetchScalarGridSpec(num...  37.6 us
    pallas_call x1, Pallas kernels, attend_backward(): pl.pallas_call(backward_kernel, grid_spec=pltpu.PrefetchScalarGridSpec(nu...  36.4 us
  transfers between devices with their start and end apart: 14, of which 8 were waited for; matrix products, arithmetic and copies ran while one was open for 4% of the time, Pallas kernels for 6%

profile of v1, /device:TPU:0, one launch (start us, length us, event | category | flops | bytes accessed | tf_op | source)
XLA Modules:
  0.0 718.5 jit_solution(10409869931939957820)
XLA Ops:
  7.2 0.8 multiply_subtract_fusion
  8.0 2.3 reduce-window.6
  10.3 0.3 slice_reduce_fusion
  10.6 0.2 reduce-window.9
  10.8 0.1 add_bitcast_fusion
  10.9 0.7 add_select_fusion.1
  11.6 7.0 fusion.11
  18.6 5.2 all-to-all-start.1
  23.8 1.2 select_reduce_fusion
  25.0 19.9 %all-to-all-done.1 = bf16[8,128,768]{2,1,0:T(8,128)(2,1)} async-done(((bf16[8,128,768]{2,1,0:T(8,128)(2,1)}), bf16[8,128,768]{2,1,0:T(8,128)(2,1)}, u32[]{:S(2)}, u32[]{:S(2)}) %all-to-all-start.1) | async-done | bytes 1572896 | tf_op jit(solution)/shard_map/all_to_all | solution.py:342
  44.9 3.3 all-to-all-start
  48.2 0.0 all-reduce.6.cloned.1.call-start
  48.3 4.8 fusion.7
  53.1 6.5 fusion.8
  59.5 0.0 all-reduce.6.cloned.1.call-update
  59.6 0.0 all-reduce.10.cloned.1.call-start
  59.6 0.6 copy-done.7
  60.2 122.6 %all-reduce.6.cloned.1.call-done.x_ref = bf16[2048,768]{1,0:T(8,128)(2,1)} async-done(((bf16[2048,768]{1,0:T(8,128)(2,1)}), bf16[2048,768]{1,0:T(8,128)(2,1)}) %all-reduce.6.cloned.1.call-update) | async-done | bytes 3145744 | tf_op jit(solution)/shard_map/psum | solution.py:346
  182.9 6.7 shard_map.119
  189.6 2.8 collective-permute-start
  192.4 1.3 collective-permute-start.1
  193.7 0.1 dynamic-slice_subtract_fusion
  193.8 0.1 copy.16
  193.9 0.1 reshape.64.index_ref
  194.0 0.7 collective-permute-done
  194.7 1.5 constant_dynamic-update-slice_fusion.2
  196.2 0.2 constant_dynamic-update-slice_fusion.1
  196.5 1.8 collective-permute-done.1
  198.2 1.7 constant_dynamic-update-slice_fusion.kv_ref
  199.9 2.1 copy-done.5
  202.1 37.6 %shard_map.120 = (bf16[2048,768]{1,0:T(8,128)(2,1)}, bf16[16,4,128,512]{3,2,1,0:T(8,128)(2,1)}, f32[192,768]{1,0:T(8,128)S(1)}) custom-call(s32[64]{0:T(128)S(1)} %reshape.64.index_ref, bf16[16,192,128]{2,1,0:T(8,128)(2,1)S(1)} %get-tuple-element.29.q_ref, bf16[48,384,128]{2,1,0:T(8,128)(2,1)} %copy-done.5, bf16[192,768]{1,0:T(8,128)(2,1)S(1)} %copy-done.3, ...), custom_call_target="tpu_custom_call" | custom-call | flops 3221225472 | bytes 62914560 | tf_op jit(solution)/shard_map/pallas_call | solution.py:114
  239.7 0.7 convert_element_type.73
  240.4 0.0 all-reduce.10.cloned.1.call-update
  240.5 0.2 all-reduce.8.cloned.1.call-start
  240.7 0.5 all-reduce.8.cloned.1.call-update
  241.2 36.4 %shard_map.121 = (bf16[16,192,128]{2,1,0:T(8,128)(2,1)S(1)}, bf16[16,384,128]{2,1,0:T(8,128)(2,1)}, f32[16,384,128]{2,1,0:T(8,128)}, bf16[16,384,128]{2,1,0:T(8,128)(2,1)}) custom-call(s32[64]{0:T(128)S(1)} %reshape.64.index_ref, bf16[16,192,128]{2,1,0:T(8,128)(2,1)S(1)} %get-tuple-element.29.q_ref, bf16[48,384,128]{2,1,0:T(8,128)(2,1)} %copy-done.5, ...), custom_call_target="tpu_custom_call" | custom-call | flops 6442450944 | bytes 94371840 | tf_op jit(solution)/shard_map/pallas_call | solution.py:191
  277.6 1.3 collective-permute-start.2
  278.9 34.7 %collective-permute-start.3 = (bf16[16,384,128]{2,1,0:T(8,128)(2,1)}, bf16[16,384,128]{2,1,0:T(8,128)(2,1)}, u32[]{:S(2)}, u32[]{:S(2)}) collective-permute-start(bf16[16,384,128]{2,1,0:T(8,128)(2,1)} %get-tuple-element.35), channel_id=1, source_target_pairs={{0,1},{1,2},{2,3},{3,4},{4,5},{5,6},{6,7},{8,9},{9,10},{10,11},{11... | collective-permute-start | bytes 4718600 | tf_op jit(solution)/shard_map/ppermute | solution.py:310
  313.7 4.4 all-to-all-start.2
  318.1 0.0 all-reduce.14.cloned.1.call-start
  318.2 10.1 %shard_map.122 = (bf16[2048,768]{1,0:T(8,128)(2,1)}, f32[576,768]{1,0:T(8,128)}) custom-call(bf16[16,192,128]{2,1,0:T(8,128)(2,1)S(1)} %get-tuple-element.32.dq_ref, f32[16,384,128]{2,1,0:T(8,128)} %get-tuple-element.33.own_ref, bf16[16,384,128]{2,1,0:T(8,128)(2,1)} %collective-permute-done.2.right_ref, ...), custom_call_target="tpu_custom_call" | custom-call | flops 3623878656 | bytes 13369344 | tf_op jit(solution)/shard_map/pallas_call | solution.py:245
  328.3 118.6 %all-reduce.8.cloned.1.call-done = bf16[2048,768]{1,0:T(8,128)(2,1)} async-done(((bf16[2048,768]{1,0:T(8,128)(2,1)}), bf16[2048,768]{1,0:T(8,128)(2,1)}) %all-reduce.8.cloned.1.call-update) | async-done | bytes 3145744 | tf_op jit(solution)/shard_map/psum | solution.py:356
  446.9 2.5 convert_element_type.76
  449.3 0.0 all-reduce.14.cloned.1.call-update
  449.4 0.0 all-reduce.12.cloned.1.call-start
  449.4 0.5 all-reduce.12.cloned.1.call-update
  449.9 0.0 reduce-scatter.5.cloned.1.call-start
  450.0 10.4 %fusion.2 = bf16[2048,1536]{1,0:T(8,128)(2,1)} fusion(bf16[1024,1536]{1,0:T(8,128)(2,1)} %bitcast.9, s32[1024]{0:T(1024)S(1)} %bitcast.51), kind=kOutput, calls=%fused_computation.3 | convolution fusion | flops 6447693824 | bytes 9441280 | tf_op jit(solution)/shard_map/dot_general | solution.py:314
  460.4 45.0 %all-reduce.14.cloned.1.call-done = bf16[576,768]{1,0:T(8,128)(2,1)} async-done(((bf16[576,768]{1,0:T(8,128)(2,1)}), bf16[576,768]{1,0:T(8,128)(2,1)}) %all-reduce.14.cloned.1.call-update) | async-done | bytes 884752 | tf_op jit(solution)/shard_map/psum | solution.py:367
  505.4 122.5 %all-reduce.12.cloned.1.call-done.dh_ref = bf16[2048,768]{1,0:T(8,128)(2,1)} async-done(((bf16[2048,768]{1,0:T(8,128)(2,1)}), bf16[2048,768]{1,0:T(8,128)(2,1)}) %all-reduce.12.cloned.1.call-update) | async-done | bytes 3145744 | tf_op jit(solution)/shard_map/psum | solution.py:366
  627.9 8.6 %shard_map.123 = (bf16[2048,768]{1,0:T(8,128)(2,1)}, f32[1,768]{1,0:T(1,128)S(1)}) custom-call(bf16[2048,768]{1,0:T(8,128)(2,1)} %all-reduce.12.cloned.1.call-done.dh_ref, bf16[2048,768]{1,0:T(8,128)(2,1)} %all-reduce.6.cloned.1.call-done.x_ref, bf16[2048,768]{1,0:T(8,128)(2,1)} %up_ref.5, f32[1,768]{1,0:T(1,128)S(1)} %reshape.65.gain_ref), custom_call_target="tpu_custom_call" | custom-call | flops 47185920 | bytes 12582912 | tf_op jit(solution)/shard_map/pallas_call | solution.py:293
  636.5 8.4 %convolution_convert_fusion = bf16[1536,768]{1,0:T(8,128)(2,1)} fusion(bf16[2048,1536]{1,0:T(8,128)(2,1)S(1)} %copy-done.9, bf16[2048,768]{1,0:T(8,128)(2,1)} %get-tuple-element.47), kind=kOutput, calls=%fused_computation.13 | convolution fusion | flops 4833017856 | bytes 11796480 | tf_op jit(solution)/shard_map/dot_general | solution.py:370
  644.9 0.0 reduce-scatter.5.cloned.1.call-update
  644.9 0.0 reduce-scatter.7.cloned.1.call-start
  645.0 0.9 convert_element_type.86
  645.9 40.8 %reduce-scatter.5.cloned.1.call-done = bf16[192,768]{1,0:T(8,128)(2,1)} async-done(((bf16[1536,768]{1,0:T(8,128)(2,1)}), bf16[192,768]{1,0:T(8,128)(2,1)}) %reduce-scatter.5.cloned.1.call-update) | async-done | bytes 294928 | tf_op jit(solution)/shard_map/reduce_scatter | solution.py:371
  686.6 1.9 copy.17
  688.5 0.0 reduce-scatter.7.cloned.1.call-update
  688.6 5.4 add_convert_fusion
  694.0 12.9 %psum.47 = bf16[768]{0:T(1024)(128)(2,1)S(1)} all-reduce(bf16[768]{0:T(1024)(128)(2,1)S(1)} %convert_reduce_fusion), channel_id=1, replica_groups=mesh['src'=4,'ctx'=8] {'ctx'}, use_global_device_ids=true, to_apply=%region_11.12 | all-reduce | flops 768 | bytes 3072 | tf_op jit(solution)/shard_map/psum | solution.py:373
  706.9 0.6 convert_element_type.82
  707.5 2.5 convert_element_type.88
  710.0 1.0 copy.18
  711.0 0.7 convert_element_type.79
  (28 shorter events, 0.1 us)
Async XLA Ops:
  7.2 4.4 copy-start
  18.6 26.3 %all-to-all-start.1 = ((bf16[8,128,768]{2,1,0:T(8,128)(2,1)}), bf16[8,128,768]{2,1,0:T(8,128)(2,1)}, u32[]{:S(2)}, u32[]{:S(2)}) async-start(bf16[8,128,768]{2,1,0:T(8,128)(2,1)} %bitcast.46), calls=%async_computation.1 | async-start | bytes 3145728 | tf_op jit(solution)/shard_map/all_to_all | solution.py:342
  44.9 8.2 %all-to-all-start = ((s32[8,1,128]{2,1,0:T(1,128)}), s32[8,1,128]{2,1,0:T(1,128)S(1)}, u32[]{:S(2)}, u32[]{:S(2)}) async-start(s32[8,1,128]{2,1,0:T(1,128)} %bitcast.2), calls=%async_computation | async-start | bytes 8192 | tf_op jit(solution)/shard_map/all_to_all | solution.py:341
  48.2 134.6 %all-reduce.6.cloned.1.call-start = ((), (), s32[]{:S(2)}) async-start(), calls=%async_computation.5 | async-start | bytes 6291456 | tf_op jit(solution)/shard_map/psum | solution.py:346
  59.5 0.7 copy-start.7
  59.5 123.3 %copy-start.2 = (bf16[768,3,192]{0,2,1:T(8,128)(2,1)S(1)}, bf16[768,3,192]{0,2,1:T(8,128)(2,1)}, u32[]{:S(2)}) copy-start(bf16[768,3,192]{0,2,1:T(8,128)(2,1)} %param.12) | copy-start | bytes 2654212
  59.6 268.7 %all-reduce.10.cloned.1.call-start = ((), (), s32[]{:S(2)}) async-start(), calls=%async_computation.7 | async-start | bytes 589824 | tf_op jit(solution)/shard_map/psum | solution.py:357
  182.9 10.9 %copy-start.8 = (s32[128,4]{0,1:T(4,128)S(1)}, s32[128,4]{0,1:T(4,128)}, u32[]{:S(2)}) copy-start(s32[128,4]{0,1:T(4,128)} %param.14) | copy-start | bytes 6148
  189.6 5.1 collective-permute-start
  192.4 5.8 collective-permute-start.1
  194.0 2.2 copy-start.4
  196.2 5.8 copy-start.3
  199.9 2.2 copy-start.5
  240.5 206.4 %all-reduce.8.cloned.1.call-start = ((), (), s32[]{:S(2)}) async-start(), calls=%async_computation.6 | async-start | bytes 6291456 | tf_op jit(solution)/shard_map/psum | solution.py:356
  277.6 40.5 %collective-permute-start.2 = (bf16[16,384,128]{2,1,0:T(8,128)(2,1)}, bf16[16,384,128]{2,1,0:T(8,128)(2,1)}, u32[]{:S(2)}, u32[]{:S(2)}) collective-permute-start(bf16[16,384,128]{2,1,0:T(8,128)(2,1)} %get-tuple-element.34), channel_id=1, source_target_pairs={{1,0},{2,1},{3,2},{4,3},{5,4},{6,5},{7,6},{9,8},{10,9},{11,10},{12... | collective-permute-start | bytes 4718600 | tf_op jit(solution)/shard_map/ppermute | solution.py:310
  278.9 39.2 %collective-permute-start.3 = (bf16[16,384,128]{2,1,0:T(8,128)(2,1)}, bf16[16,384,128]{2,1,0:T(8,128)(2,1)}, u32[]{:S(2)}, u32[]{:S(2)}) collective-permute-start(bf16[16,384,128]{2,1,0:T(8,128)(2,1)} %get-tuple-element.35), channel_id=1, source_target_pairs={{0,1},{1,2},{2,3},{3,4},{4,5},{5,6},{6,7},{8,9},{9,10},{10,11},{11... | collective-permute-start | bytes 4718600 | tf_op jit(solution)/shard_map/ppermute | solution.py:310
  313.7 136.3 %all-to-all-start.2 = ((bf16[8,128,1536]{2,1,0:T(8,128)(2,1)}), bf16[8,128,1536]{2,1,0:T(8,128)(2,1)}, u32[]{:S(2)}, u32[]{:S(2)}) async-start(bf16[8,128,1536]{2,1,0:T(8,128)(2,1)} %bitcast.44), calls=%async_computation.2 | async-start | bytes 6291456 | tf_op jit(solution)/shard_map/all_to_all | solution.py:344
  318.1 187.3 %all-reduce.14.cloned.1.call-start = ((), (), s32[]{:S(2)}) async-start(), calls=%async_computation.9 | async-start | bytes 1769472 | tf_op jit(solution)/shard_map/psum | solution.py:367
  449.4 178.6 %all-reduce.12.cloned.1.call-start = ((), (), s32[]{:S(2)}) async-start(), calls=%async_computation.8 | async-start | bytes 6291456 | tf_op jit(solution)/shard_map/psum | solution.py:366
  449.9 236.7 %reduce-scatter.5.cloned.1.call-start = ((), (), s32[]{:S(2)}) async-start(), calls=%async_computation.10 | async-start | bytes 2654208 | tf_op jit(solution)/shard_map/reduce_scatter | solution.py:371
  627.9 8.6 %copy-start.9 = (bf16[2048,1536]{1,0:T(8,128)(2,1)S(1)}, bf16[2048,1536]{1,0:T(8,128)(2,1)}, u32[]{:S(2)}) copy-start(bf16[2048,1536]{1,0:T(8,128)(2,1)} %fusion.2) | copy-start | bytes 18874372
  636.5 8.5 %copy-start.6 = (bf16[192,768]{1,0:T(8,128)(2,1)S(1)}, bf16[192,768]{1,0:T(8,128)(2,1)}, u32[]{:S(2)}) copy-start(bf16[192,768]{1,0:T(8,128)(2,1)} %all-reduce.10.cloned.1.call-done) | copy-start | bytes 884740
  644.9 65.1 %reduce-scatter.7.cloned.1.call-start = ((), (), s32[]{:S(2)}) async-start(), calls=%async_computation.11 | async-start | bytes 491520
  688.5 23.2 %copy-start.1 = (bf16[1024,1536]{1,0:T(8,128)(2,1)S(1)}, bf16[1024,1536]{1,0:T(8,128)(2,1)}, u32[]{:S(2)}) copy-start(bf16[1024,1536]{1,0:T(8,128)(2,1)} %param.8) | copy-start | bytes 9437188
Sparse Core Ops, SparseCore 0:
  59.7 123.1 all-reduce.5
  240.6 82.2 all-reduce.9
  325.2 121.5 all-reduce.7
  450.5 54.8 all-reduce.13
  507.6 120.2 all-reduce.11
  645.1 41.5 reduce-scatter.4
  689.0 20.5 reduce-scatter.6

commit v2 on v1

--- a/solution.py
+++ b/solution.py
@@ -1,5 +1,3 @@
-import functools
-
 import jax
 import jax.numpy as jnp
 from jax import lax
@@ -310,6 +308,22 @@
     return lax.ppermute(value, axis, [(source, source + steps) for source in range(initial, last)])
 
 
+def exchange(value, axis):
+    return lax.all_to_all(value, axis, split_axis=0, concat_axis=0, tiled=True)
+
+
+def sum_scatter(value, axis):
+    count = lax.axis_size(axis)
+    terms = exchange(value.astype(BF16).reshape(count, -1, value.shape[-1]), axis)
+    return jnp.sum(terms.astype(F32), 0)
+
+
+def sum_all(value, axis):
+    count = lax.axis_size(axis)
+    share = sum_scatter(value, axis).astype(BF16)
+    return exchange(jnp.broadcast_to(share, (count,) + share.shape), axis).reshape(value.shape)
+
+
 def mm(a, b):
     return jnp.dot(a, b, preferred_element_type=F32).astype(BF16)
 
@@ -335,16 +349,13 @@
     send_pos = jnp.max(jnp.where(in_slot, local_pos[None, :], -1), 1)
     pick = in_slot.astype(BF16)
     send_proj = mm(pick, mm(embeddings, in_weight))
-    swap = functools.partial(
-        lax.all_to_all, axis_name="ctx", split_axis=0, concat_axis=0, tiled=True
-    )
-    got_pos = swap(send_pos.reshape(shards, capacity)).reshape(produced)
-    got_proj = swap(send_proj.reshape(shards, capacity, -1)).reshape(produced, -1)
+    got_pos = exchange(send_pos.reshape(shards, capacity), "ctx").reshape(produced)
+    got_proj = exchange(send_proj.reshape(shards, capacity, -1), "ctx").reshape(produced, -1)
     send_rows, got_proj = lax.optimization_barrier((mm(pick, embeddings), got_proj))
-    got_rows = swap(send_rows.reshape(shards, capacity, -1)).reshape(produced, -1)
+    got_rows = exchange(send_rows.reshape(shards, capacity, -1), "ctx").reshape(produced, -1)
     place = (got_pos[None, :] == jnp.arange(seq_dev, dtype=jnp.int32)[:, None]).astype(BF16)
     start_x = lax.psum(mm(place, got_proj), "src")
-    slide = mm(place, got_rows)
+    start_x, slide = lax.optimization_barrier((start_x, mm(place, got_rows)))
 
     hidden, q, kv = project_rows(start_x, gain, wt, cols)
     ext_kv = jnp.concatenate(
@@ -354,31 +365,29 @@
     index = (my_lists - (my_shard - 1) * per_shard).reshape(-1)
     part, probs, out_part = attend_forward(index, q, ext_kv, out_weight, upstream)
     attn_total = lax.psum(part, "src")
-    out_sum = lax.psum(out_part.astype(BF16), "ctx")
     dq, before, own, after = attend_backward(index, q, ext_kv, out_weight, upstream, probs)
     from_right = from_behind(before, "ctx", -1)
     from_left = from_behind(after, "ctx", 1)
     hidden_part, qkv_part = gradient_products(dq, own, from_right, from_left, hidden, wt)
-    hidden_part, qkv_part, attn_total, out_sum = lax.optimization_barrier(
-        (hidden_part, qkv_part, attn_total, out_sum)
-    )
+    weight_part = jnp.concatenate([qkv_part, out_part], axis=0)
+    hidden_part, attn_total = lax.optimization_barrier((hidden_part, attn_total))
+    d_hidden = lax.psum(hidden_part, "src")
     encoded = (start_x.astype(F32) + attn_total.astype(F32)).astype(BF16)
-    d_hidden = lax.psum(hidden_part, "src")
-    qkv_sum = lax.psum(qkv_part.astype(BF16), "ctx")
-    d_hidden, qkv_sum, slide = lax.optimization_barrier((d_hidden, qkv_sum, slide))
+    weight_sum = sum_all(weight_part, "ctx").astype(F32)
+    qkv_grad = weight_sum[: 3 * cols].T.reshape(model_dim, 3, cols)
+    out_grad = weight_sum[3 * cols :]
+    d_hidden, qkv_grad, out_grad, encoded = lax.optimization_barrier(
+        (d_hidden, qkv_grad, out_grad, encoded)
+    )
     d_start, gain_part = norm_back(d_hidden, start_x, upstream, gain)
+    gain_terms = exchange(jnp.broadcast_to(gain_part.astype(BF16), (shards, model_dim)), "ctx")
+    gain_grad = jnp.sum(gain_terms.astype(F32), 0)
     in_part = lax.dot_general(slide, d_start, (((0,), (0,)), ((), ())), preferred_element_type=F32)
-    row_share = lax.psum_scatter(in_part.astype(BF16), "ctx", scatter_dimension=0, tiled=True)
-    in_grad = lax.psum_scatter(row_share, "src", scatter_dimension=1, tiled=True)
-    gain_sum = lax.psum(gain_part.astype(BF16), "ctx").reshape(model_dim)
-    qkv_grad = qkv_sum.T.reshape(model_dim, 3, cols)
-    return (
-        encoded,
-        in_grad.astype(F32),
-        gain_sum.astype(F32),
-        qkv_grad.astype(F32),
-        out_sum.astype(F32),
-    )
+    row_share = sum_scatter(in_part, "ctx")
+    sources = lax.axis_size("src")
+    col_parts = jnp.moveaxis(row_share.reshape(row_share.shape[0], sources, -1), 1, 0)
+    in_grad = sum_scatter(col_parts.reshape(-1, col_parts.shape[-1]), "src")
+    return (encoded, in_grad, gain_grad, qkv_grad, out_grad)
 
 
 def solution(mesh):

time: 719 us -> 600 us (0.83)
  waiting for transfers between devices: 473 us -> 328 us
  starting transfers between devices: 53.5 us -> 67.2 us
  blocking collectives: 12.9 us -> 20.2 us
    all_to_all x3 -> x7, waiting for transfers between devices: 19.9 us -> 99.6 us  [exchange(): return lax.all_to_all(value, axis, split_axis=0, concat_axis=0, tiled=True)]
    psum x1, waiting for transfers between devices: 119 us -> 64.3 us  [local(): attn_total = lax.psum(part, 'src')]
    psum x1, waiting for transfers between devices: 123 us -> 76.8 us  [local(): d_hidden = lax.psum(hidden_part, 'src')]
    psum x2 -> x0, waiting for transfers between devices: 45 us -> none  [the longest x1 45 us: local(): qkv_sum = lax.psum(qkv_part.astype(BF16), 'ctx')]
    psum x1, waiting for transfers between devices: 123 us -> 81.4 us  [local(): start_x = lax.psum(mm(place, got_proj), 'src')]
    reduce_scatter x1 -> x0, waiting for transfers between devices: 40.8 us -> none  [local(): lax.psum_scatter(in_part.astype(BF16), 'ctx', scatter_dimension=0, tiled=...]
    all_to_all x0 -> x1, blocking collectives: none -> 20.2 us  [exchange(): return lax.all_to_all(value, axis, split_axis=0, concat_axis=0, tiled=True)]
    all_to_all x3 -> x7, starting transfers between devices: 12.9 us -> 27.9 us  [exchange(): return lax.all_to_all(value, axis, split_axis=0, concat_axis=0, tiled=True)]
  transfers between devices with their start and end apart: 14 -> 14, of which waited for: 8 -> 12; matrix products, arithmetic and copies ran while one was open for 4% -> 7% of each run, Pallas kernels for 6% -> 8%
where the time goes in v2:
time: 600 us; the launch traced here: 599 us
  waiting for transfers between devices  328 us (55%)
  Pallas kernels  98.7 us (16%)
  starting transfers between devices  67.2 us (11%)
  matrix products  38.1 us (6%)
  blocking collectives  20.2 us (3%)
  other arithmetic  18.5 us (3%)
  local copies, waits for them, and re-layouts  14.8 us (2%)
  between operations  14 us (2%)
    all_to_all x7, waiting for transfers between devices, exchange(): return lax.all_to_all(value, axis, split_axis=0, concat_axis=0, tiled=True)  99.6 us
    psum x1, waiting for transfers between devices, local(): start_x = lax.psum(mm(place, got_proj), 'src')  81.4 us
    psum x1, waiting for transfers between devices, local(): d_hidden = lax.psum(hidden_part, 'src')  76.8 us
    psum x1, waiting for transfers between devices, local(): attn_total = lax.psum(part, 'src')  64.3 us
    ppermute x4, starting transfers between devices, from_behind(): lax.ppermute(value, axis, [(source, source + steps) for source in range(i...  39 us
    pallas_call x1, Pallas kernels, attend_forward(): pl.pallas_call(forward_kernel, grid_spec=pltpu.PrefetchScalarGridSpec(num...  37.6 us
    pallas_call x1, Pallas kernels, attend_backward(): pl.pallas_call(backward_kernel, grid_spec=pltpu.PrefetchScalarGridSpec(nu...  36.4 us
    dot_general x4, matrix products, mm(): return jnp.dot(a, b, preferred_element_type=F32).astype(BF16)  28.8 us
  transfers between devices with their start and end apart: 14, of which 12 were waited for; matrix products, arithmetic and copies ran while one was open for 7% of the time, Pallas kernels for 8%

profile of v2, /device:TPU:0, one launch (start us, length us, event | category | flops | bytes accessed | tf_op | source)
XLA Modules:
  0.0 599.1 jit_solution(13133920381328487468)
XLA Ops:
  7.2 0.8 multiply_subtract_fusion
  8.0 2.3 reduce-window.6
  10.3 0.3 slice_reduce_fusion
  10.6 0.2 reduce-window.9
  10.9 0.7 add_select_fusion.1
  11.6 7.0 %fusion.11 = bf16[1024,768]{1,0:T(8,128)(2,1)} fusion(s32[1024]{0:T(1024)S(1)} %add_select_fusion.1, bf16[1024,1536]{1,0:T(8,128)(2,1)S(1)} %copy-done, bf16[1536,768]{1,0:T(8,128)(2,1)} %param.10), kind=kOutput, calls=%fused_computation.16 | convolution fusion | flops 4029153280 | bytes 7081984 | tf_op jit(solution)/shard_map/dot_general | solution.py:328
  18.6 5.2 all-to-all-start.1
  23.8 1.2 select_reduce_fusion
  25.0 19.9 %all-to-all-done.1 = bf16[8,128,768]{2,1,0:T(8,128)(2,1)} async-done(((bf16[8,128,768]{2,1,0:T(8,128)(2,1)}), bf16[8,128,768]{2,1,0:T(8,128)(2,1)}, u32[]{:S(2)}, u32[]{:S(2)}) %all-to-all-start.1) | async-done | bytes 1572896 | tf_op jit(solution)/shard_map/all_to_all | solution.py:312
  44.9 3.3 all-to-all-start
  48.2 4.8 fusion.7
  53.0 4.5 all-to-all-start.2
  57.5 6.5 %fusion.8 = bf16[2048,768]{1,0:T(8,128)(2,1)} fusion(bf16[1024,768]{1,0:T(8,128)(2,1)} %bitcast.5, s32[1024]{0:T(1024)S(1)} %bitcast.56), kind=kOutput, calls=%fused_computation.12 | convolution fusion | flops 3224895488 | bytes 4722688 | tf_op jit(solution)/shard_map/dot_general | solution.py:328
  64.0 0.2 all-reduce.6.cloned.1.call-start
  64.3 0.4 copy-done.6
  64.7 30.7 %all-to-all-done.2 = bf16[8,128,1536]{2,1,0:T(8,128)(2,1)} async-done(((bf16[8,128,1536]{2,1,0:T(8,128)(2,1)}), bf16[8,128,1536]{2,1,0:T(8,128)(2,1)}, u32[]{:S(2)}, u32[]{:S(2)}) %all-to-all-start.2) | async-done | bytes 3145760 | tf_op jit(solution)/shard_map/all_to_all | solution.py:312
  95.4 10.5 %fusion.2 = bf16[2048,1536]{1,0:T(8,128)(2,1)} fusion(bf16[1024,1536]{1,0:T(8,128)(2,1)} %bitcast.7, s32[1024]{0:T(1024)S(1)} %bitcast.57), kind=kOutput, calls=%fused_computation.3 | convolution fusion | flops 6447693824 | bytes 9441280 | tf_op jit(solution)/shard_map/dot_general | solution.py:328
  105.9 81.4 %all-reduce.4.cloned.1.call-done.x_ref = bf16[2048,768]{1,0:T(8,128)(2,1)} async-done(((bf16[2048,768]{1,0:T(8,128)(2,1)}), bf16[2048,768]{1,0:T(8,128)(2,1)}) %all-reduce.4.cloned.1.call-update) | async-done | bytes 3145744 | tf_op jit(solution)/shard_map/psum | solution.py:357
  187.3 6.7 %shard_map.119 = (bf16[2048,768]{1,0:T(8,128)(2,1)}, bf16[16,192,128]{2,1,0:T(8,128)(2,1)S(1)}, bf16[16,384,128]{2,1,0:T(8,128)(2,1)}) custom-call(bf16[2048,768]{1,0:T(8,128)(2,1)} %all-reduce.4.cloned.1.call-done.x_ref, f32[1,768]{1,0:T(1,128)S(1)} %reshape.85.gain_ref, bf16[576,768]{1,0:T(8,128)(2,1)S(1)} %bitcast.46), custom_call_target="tpu_custom_call" | custom-call | flops 1811939328 | bytes 9437184 | tf_op jit(solution)/shard_map/pallas_call | solution.py:54
  194.1 2.9 collective-permute-start
  196.9 1.3 collective-permute-start.1
  198.3 0.1 copy.23
  198.4 0.1 reshape.79.index_ref
  198.5 0.6 collective-permute-done
  199.1 1.5 constant_dynamic-update-slice_fusion.2
  200.7 0.2 constant_dynamic-update-slice_fusion.1
  200.9 1.8 collective-permute-done.1
  202.7 1.7 constant_dynamic-update-slice_fusion.kv_ref
  204.4 2.1 copy-done.5
  206.5 37.6 %shard_map.120 = (bf16[2048,768]{1,0:T(8,128)(2,1)}, bf16[16,4,128,512]{3,2,1,0:T(8,128)(2,1)}, f32[192,768]{1,0:T(8,128)S(1)}) custom-call(s32[64]{0:T(128)S(1)} %reshape.79.index_ref, bf16[16,192,128]{2,1,0:T(8,128)(2,1)S(1)} %get-tuple-element.32.q_ref, bf16[48,384,128]{2,1,0:T(8,128)(2,1)} %copy-done.5, bf16[192,768]{1,0:T(8,128)(2,1)S(1)} %copy-done.3, ...), custom_call_target="tpu_custom_call" | custom-call | flops 3221225472 | bytes 62914560 | tf_op jit(solution)/shard_map/pallas_call | solution.py:112
  244.2 36.4 %shard_map.121 = (bf16[16,192,128]{2,1,0:T(8,128)(2,1)S(1)}, bf16[16,384,128]{2,1,0:T(8,128)(2,1)}, f32[16,384,128]{2,1,0:T(8,128)}, bf16[16,384,128]{2,1,0:T(8,128)(2,1)}) custom-call(s32[64]{0:T(128)S(1)} %reshape.79.index_ref, bf16[16,192,128]{2,1,0:T(8,128)(2,1)S(1)} %get-tuple-element.32.q_ref, bf16[48,384,128]{2,1,0:T(8,128)(2,1)} %copy-done.5, ...), custom_call_target="tpu_custom_call" | custom-call | flops 6442450944 | bytes 94371840 | tf_op jit(solution)/shard_map/pallas_call | solution.py:189
  280.6 1.3 collective-permute-start.2
  281.9 33.6 %collective-permute-start.3 = (bf16[16,384,128]{2,1,0:T(8,128)(2,1)}, bf16[16,384,128]{2,1,0:T(8,128)(2,1)S(1)}, u32[]{:S(2)}, u32[]{:S(2)}) collective-permute-start(bf16[16,384,128]{2,1,0:T(8,128)(2,1)} %get-tuple-element.38), channel_id=1, source_target_pairs={{0,1},{1,2},{2,3},{3,4},{4,5},{5,6},{6,7},{8,9},{9,10},{10,11},{11... | collective-permute-start | bytes 4718600 | tf_op jit(solution)/shard_map/ppermute | solution.py:308
  315.5 1.1 collective-permute-done.2.right_ref
  316.6 2.0 collective-permute-done.3.left_ref
  318.6 1.2 copy-done.9
  319.8 10.1 %shard_map.122 = (bf16[2048,768]{1,0:T(8,128)(2,1)}, f32[576,768]{1,0:T(8,128)}) custom-call(bf16[16,192,128]{2,1,0:T(8,128)(2,1)S(1)} %get-tuple-element.35.dq_ref, f32[16,384,128]{2,1,0:T(8,128)} %get-tuple-element.36.own_ref, bf16[16,384,128]{2,1,0:T(8,128)(2,1)} %copy-done.8, bf16[16,384,128]{2,1,0:T(8,128)(2,1)} %copy-done.9, ...), custom_call_target="tpu_custom_call" | custom-call | flops 3623878656 | bytes 13369344 | tf_op jit(solution)/shard_map/pallas_call | solution.py:243
  329.8 64.3 %all-reduce.6.cloned.1.call-done = bf16[2048,768]{1,0:T(8,128)(2,1)} async-done(((bf16[2048,768]{1,0:T(8,128)(2,1)}), bf16[2048,768]{1,0:T(8,128)(2,1)}) %all-reduce.6.cloned.1.call-update) | async-done | bytes 3145744 | tf_op jit(solution)/shard_map/psum | solution.py:367
  394.2 1.6 convert.8
  395.9 20.2 %all_to_all.45 = bf16[8,96,768]{2,1,0:T(8,128)(2,1)S(1)} all-to-all(bf16[8,96,768]{2,1,0:T(8,128)(2,1)S(1)} %bitcast.48), channel_id=1, replica_groups=mesh['src'=4,'ctx'=8] {'ctx'}, dimensions={0} | all-to-all | bytes 2359296 | tf_op jit(solution)/shard_map/all_to_all | solution.py:312
  416.1 0.2 reduce_sum.52
  416.3 1.1 broadcast_in_dim.33
  417.3 3.8 all-to-all-start.4
  421.1 5.4 add_convert_fusion
  426.5 11.2 %all-to-all-done.4 = bf16[8,96,768]{2,1,0:T(8,128)(2,1)S(1)} async-done(((bf16[8,96,768]{2,1,0:T(8,128)(2,1)}), bf16[8,96,768]{2,1,0:T(8,128)(2,1)S(1)}, u32[]{:S(2)}, u32[]{:S(2)}) %all-to-all-start.4) | async-done | bytes 1179680 | tf_op jit(solution)/shard_map/all_to_all | solution.py:312
  437.7 1.4 slice.25
  439.0 0.9 slice.26
  439.9 76.8 %all-reduce.8.cloned.1.call-done.dh_ref = bf16[2048,768]{1,0:T(8,128)(2,1)} async-done(((bf16[2048,768]{1,0:T(8,128)(2,1)}), bf16[2048,768]{1,0:T(8,128)(2,1)}) %all-reduce.8.cloned.1.call-update) | async-done | bytes 3145744 | tf_op jit(solution)/shard_map/psum | solution.py:374
  516.6 7.9 %shard_map.123 = (bf16[2048,768]{1,0:T(8,128)(2,1)}, f32[1,768]{1,0:T(1,128)S(1)}) custom-call(bf16[2048,768]{1,0:T(8,128)(2,1)} %all-reduce.8.cloned.1.call-done.dh_ref, bf16[2048,768]{1,0:T(8,128)(2,1)} %all-reduce.4.cloned.1.call-done.x_ref, bf16[2048,768]{1,0:T(8,128)(2,1)} %up_ref.5, f32[1,768]{1,0:T(1,128)S(1)} %reshape.85.gain_ref), custom_call_target="tpu_custom_call" | custom-call | flops 47185920 | bytes 12582912 | tf_op jit(solution)/shard_map/pallas_call | solution.py:291
  524.5 9.3 %convolution_convert_fusion = bf16[1536,768]{1,0:T(8,128)(2,1)} fusion(bf16[2048,1536]{1,0:T(8,128)(2,1)} %fusion.2, bf16[2048,768]{1,0:T(8,128)(2,1)} %get-tuple-element.49), kind=kOutput, calls=%fused_computation.13 | convolution fusion | flops 4833017856 | bytes 11796480 | tf_op jit(solution)/shard_map/dot_general | solution.py:385
  533.8 4.4 all-to-all-start.5
  538.2 0.5 broadcast.42
  538.7 1.0 reduce.7
  539.7 0.6 reshape.91
  540.3 27.3 %all-to-all-done.5 = bf16[8,192,768]{2,1,0:T(8,128)(2,1)} async-done(((bf16[8,192,768]{2,1,0:T(8,128)(2,1)}), bf16[8,192,768]{2,1,0:T(8,128)(2,1)}, u32[]{:S(2)}, u32[]{:S(2)}) %all-to-all-start.5) | async-done | bytes 2359328 | tf_op jit(solution)/shard_map/all_to_all | solution.py:312
  567.6 3.3 all-to-all-start.7
  571.0 2.8 reduce_sum.53
  573.7 1.3 convert_element_type.81
  575.1 0.8 copy.24
  575.9 3.5 all-to-all-start.6
  579.3 0.6 reshape.92
  580.0 1.3 convert_reduce_fusion.1
  581.3 10.6 %all-to-all-done.6 = bf16[4,192,192]{2,1,0:T(8,128)(2,1)S(1)} async-done(((bf16[4,192,192]{2,1,0:T(8,128)(2,1)}), bf16[4,192,192]{2,1,0:T(8,128)(2,1)S(1)}, u32[]{:S(2)}, u32[]{:S(2)}) %all-to-all-start.6) | async-done | bytes 294944 | tf_op jit(solution)/shard_map/all_to_all | solution.py:312
  591.9 0.7 convert_reduce_fusion
  (33 shorter events, 0.5 us)
Async XLA Ops:
  7.2 4.4 copy-start
  18.6 26.3 %all-to-all-start.1 = ((bf16[8,128,768]{2,1,0:T(8,128)(2,1)}), bf16[8,128,768]{2,1,0:T(8,128)(2,1)}, u32[]{:S(2)}, u32[]{:S(2)}) async-start(bf16[8,128,768]{2,1,0:T(8,128)(2,1)} %bitcast.52), calls=%async_computation.1 | async-start | bytes 3145728 | tf_op jit(solution)/shard_map/all_to_all | solution.py:312
  44.9 8.1 %all-to-all-start = ((s32[8,1,128]{2,1,0:T(1,128)}), s32[8,1,128]{2,1,0:T(1,128)S(1)}, u32[]{:S(2)}, u32[]{:S(2)}) async-start(s32[8,1,128]{2,1,0:T(1,128)} %bitcast.2), calls=%async_computation | async-start | bytes 8192 | tf_op jit(solution)/shard_map/all_to_all | solution.py:312
  53.0 42.4 %all-to-all-start.2 = ((bf16[8,128,1536]{2,1,0:T(8,128)(2,1)}), bf16[8,128,1536]{2,1,0:T(8,128)(2,1)}, u32[]{:S(2)}, u32[]{:S(2)}) async-start(bf16[8,128,1536]{2,1,0:T(8,128)(2,1)} %bitcast.49), calls=%async_computation.2 | async-start | bytes 6291456 | tf_op jit(solution)/shard_map/all_to_all | solution.py:312
  57.5 129.9 %all-reduce.4.cloned.1.call-start = ((), (), s32[]{:S(2)}) async-start(), calls=%async_computation.8 | async-start | bytes 6291456 | tf_op jit(solution)/shard_map/psum | solution.py:357
  64.0 0.7 copy-start.6
  64.0 330.1 %all-reduce.6.cloned.1.call-start = ((), (), s32[]{:S(2)}) async-start(), calls=%async_computation.9 | async-start | bytes 6291456 | tf_op jit(solution)/shard_map/psum | solution.py:367
  95.3 92.0 %copy-start.2 = (bf16[768,3,192]{0,2,1:T(8,128)(2,1)S(1)}, bf16[768,3,192]{0,2,1:T(8,128)(2,1)}, u32[]{:S(2)}) copy-start(bf16[768,3,192]{0,2,1:T(8,128)(2,1)} %param.12) | copy-start | bytes 2654212
  187.3 10.9 %copy-start.7 = (s32[128,4]{0,1:T(4,128)S(1)}, s32[128,4]{0,1:T(4,128)}, u32[]{:S(2)}) copy-start(s32[128,4]{0,1:T(4,128)} %param.14) | copy-start | bytes 6148
  194.1 5.1 collective-permute-start
  196.9 5.8 collective-permute-start.1
  198.5 2.2 copy-start.4
  200.7 5.8 copy-start.3
  204.4 2.1 copy-start.5
  244.1 272.5 %all-reduce.8.cloned.1.call-start = ((), (), s32[]{:S(2)}) async-start(), calls=%async_computation.10 | async-start | bytes 6291456 | tf_op jit(solution)/shard_map/psum | solution.py:374
  280.6 36.0 %collective-permute-start.2 = (bf16[16,384,128]{2,1,0:T(8,128)(2,1)}, bf16[16,384,128]{2,1,0:T(8,128)(2,1)S(1)}, u32[]{:S(2)}, u32[]{:S(2)}) collective-permute-start(bf16[16,384,128]{2,1,0:T(8,128)(2,1)} %get-tuple-element.37), channel_id=1, source_target_pairs={{1,0},{2,1},{3,2},{4,3},{5,4},{6,5},{7,6},{9,8},{10,9},{11,10},{12... | collective-permute-start | bytes 4718600 | tf_op jit(solution)/shard_map/ppermute | solution.py:308
  281.9 36.8 %collective-permute-start.3 = (bf16[16,384,128]{2,1,0:T(8,128)(2,1)}, bf16[16,384,128]{2,1,0:T(8,128)(2,1)S(1)}, u32[]{:S(2)}, u32[]{:S(2)}) collective-permute-start(bf16[16,384,128]{2,1,0:T(8,128)(2,1)} %get-tuple-element.38), channel_id=1, source_target_pairs={{0,1},{1,2},{2,3},{3,4},{4,5},{5,6},{6,7},{8,9},{9,10},{10,11},{11... | collective-permute-start | bytes 4718600 | tf_op jit(solution)/shard_map/ppermute | solution.py:308
  316.6 2.1 copy-start.8
  318.6 1.2 copy-start.9
  417.3 20.3 %all-to-all-start.4 = ((bf16[8,96,768]{2,1,0:T(8,128)(2,1)}), bf16[8,96,768]{2,1,0:T(8,128)(2,1)S(1)}, u32[]{:S(2)}, u32[]{:S(2)}) async-start(bf16[8,96,768]{2,1,0:T(8,128)(2,1)} %broadcast_in_dim.33), calls=%async_computation.4 | async-start | bytes 2359296 | tf_op jit(solution)/shard_map/all_to_all | solution.py:312
  533.8 33.8 %all-to-all-start.5 = ((bf16[8,192,768]{2,1,0:T(8,128)(2,1)}), bf16[8,192,768]{2,1,0:T(8,128)(2,1)}, u32[]{:S(2)}, u32[]{:S(2)}) async-start(bf16[8,192,768]{2,1,0:T(8,128)(2,1)} %bitcast.50), calls=%async_computation.5 | async-start | bytes 4718592 | tf_op jit(solution)/shard_map/all_to_all | solution.py:312
  538.2 54.4 %copy-start.1 = (bf16[1024,1536]{1,0:T(8,128)(2,1)S(1)}, bf16[1024,1536]{1,0:T(8,128)(2,1)}, u32[]{:S(2)}) copy-start(bf16[1024,1536]{1,0:T(8,128)(2,1)} %param.8) | copy-start | bytes 9437188
  567.6 8.2 %all-to-all-start.7 = ((bf16[8,2,384]{2,1,0:T(2,128)(2,1)}), bf16[8,2,384]{2,1,0:T(2,128)(2,1)S(1)}, u32[]{:S(2)}, u32[]{:S(2)}) async-start(bf16[8,2,384]{2,1,0:T(2,128)(2,1)} %reshape.91), calls=%async_computation.7 | async-start | bytes 24576 | tf_op jit(solution)/shard_map/all_to_all | solution.py:312
  575.9 16.0 %all-to-all-start.6 = ((bf16[4,192,192]{2,1,0:T(8,128)(2,1)}), bf16[4,192,192]{2,1,0:T(8,128)(2,1)S(1)}, u32[]{:S(2)}, u32[]{:S(2)}) async-start(bf16[4,192,192]{2,1,0:T(8,128)(2,1)} %copy.24), calls=%async_computation.6 | async-start | bytes 786432 | tf_op jit(solution)/shard_map/all_to_all | solution.py:312
Sparse Core Ops, SparseCore 0:
  64.1 123.1 all-reduce.3
  244.3 149.8 all-reduce.5
  396.5 120.0 all-reduce.7

commit v3 on v2

--- a/solution.py
+++ b/solution.py
@@ -353,14 +353,35 @@
     got_proj = exchange(send_proj.reshape(shards, capacity, -1), "ctx").reshape(produced, -1)
     send_rows, got_proj = lax.optimization_barrier((mm(pick, embeddings), got_proj))
     got_rows = exchange(send_rows.reshape(shards, capacity, -1), "ctx").reshape(produced, -1)
-    place = (got_pos[None, :] == jnp.arange(seq_dev, dtype=jnp.int32)[:, None]).astype(BF16)
-    start_x = lax.psum(mm(place, got_proj), "src")
-    start_x, slide = lax.optimization_barrier((start_x, mm(place, got_rows)))
-
-    hidden, q, kv = project_rows(start_x, gain, wt, cols)
+    half = seq_dev // 2
+    rows_low = jnp.arange(half, dtype=jnp.int32)[:, None]
+    place_low = (got_pos[None, :] == rows_low).astype(BF16)
+    place_high = (got_pos[None, :] == rows_low + half).astype(BF16)
+    x_low = lax.psum(mm(place_low, got_proj), "src")
+    placed_high, x_low = lax.optimization_barrier((mm(place_high, got_proj), x_low))
+    x_high = lax.psum(placed_high, "src")
+    hidden_low, q_low, kv_low = project_rows(x_low, gain, wt, cols)
+    left_low = from_behind(kv_low, "ctx", 1)
+    right_low = from_behind(kv_low, "ctx", -1)
+    place = jnp.concatenate([place_low, place_high], axis=0)
+    x_high, slide, left_low, right_low = lax.optimization_barrier(
+        (x_high, mm(place, got_rows), left_low, right_low)
+    )
+    hidden_high, q_high, kv_high = project_rows(x_high, gain, wt, cols)
     ext_kv = jnp.concatenate(
-        [from_behind(kv, "ctx", 1), kv, from_behind(kv, "ctx", -1)], axis=0
-    )
+        [
+            left_low,
+            from_behind(kv_high, "ctx", 1),
+            kv_low,
+            kv_high,
+            right_low,
+            from_behind(kv_high, "ctx", -1),
+        ],
+        axis=0,
+    )
+    q = jnp.concatenate([q_low, q_high], axis=0)
+    hidden = jnp.concatenate([hidden_low, hidden_high], axis=0)
+    start_x = jnp.concatenate([x_low, x_high], axis=0)
     my_lists = lax.dynamic_slice_in_dim(neighbors, my_shard * per_shard, per_shard, 0)
     index = (my_lists - (my_shard - 1) * per_shard).reshape(-1)
     part, probs, out_part = attend_forward(index, q, ext_kv, out_weight, upstream)
@@ -381,9 +402,10 @@
     )
     d_start, gain_part = norm_back(d_hidden, start_x, upstream, gain)
     gain_terms = exchange(jnp.broadcast_to(gain_part.astype(BF16), (shards, model_dim)), "ctx")
+    in_part = dot(slide, d_start, 0, 0).astype(BF16)
+    in_part, gain_terms = lax.optimization_barrier((in_part, gain_terms))
+    row_share = sum_scatter(in_part, "ctx")
     gain_grad = jnp.sum(gain_terms.astype(F32), 0)
-    in_part = lax.dot_general(slide, d_start, (((0,), (0,)), ((), ())), preferred_element_type=F32)
-    row_share = sum_scatter(in_part, "ctx")
     sources = lax.axis_size("src")
     col_parts = jnp.moveaxis(row_share.reshape(row_share.shape[0], sources, -1), 1, 0)
     in_grad = sum_scatter(col_parts.reshape(-1, col_parts.shape[-1]), "src")

time: 600 us -> 604 us (level)
  blocking collectives: 20.2 us -> 54.3 us
  waiting for transfers between devices: 328 us -> 306 us
  starting transfers between devices: 67.2 us -> 50.7 us
    all_to_all x7 -> x6, waiting for transfers between devices: 99.6 us -> 41.4 us  [exchange(): return lax.all_to_all(value, axis, split_axis=0, concat_axis=0, tiled=True)]
    psum x1 -> x2, waiting for transfers between devices: 81.4 us -> 124 us  [the longest x1 64.6 us: local(): x_low = lax.psum(mm(place_low, got_proj), 'src')]
    all_to_all x1 -> x2, blocking collectives: 20.2 us -> 54.3 us  [exchange(): return lax.all_to_all(value, axis, split_axis=0, concat_axis=0, tiled=True)]
    ppermute x4 -> x6, starting transfers between devices: 39 us -> 26 us  [from_behind(): lax.ppermute(value, axis, [(source, source + steps) for source in range(i...]
    all_to_all x7 -> x6, starting transfers between devices: 27.9 us -> 24.3 us  [exchange(): return lax.all_to_all(value, axis, split_axis=0, concat_axis=0, tiled=True)]
    dot_general x4 -> x5, matrix products: 28.8 us -> 31 us  [mm(): return jnp.dot(a, b, preferred_element_type=F32).astype(BF16)]
  transfers between devices with their start and end apart: 14 -> 16, of which waited for: 12 -> 9; matrix products, arithmetic and copies ran while one was open for 7% -> 9% of each run, Pallas kernels for 8% -> 8%
where the time goes in v3:
time: 604 us; the launch traced here: 603 us
  waiting for transfers between devices  306 us (51%)
  Pallas kernels  100 us (17%)
  blocking collectives  54.3 us (9%)
  starting transfers between devices  50.7 us (8%)
  matrix products  40.3 us (7%)
  local copies, waits for them, and re-layouts  19.6 us (3%)
  other arithmetic  17.2 us (3%)
  between operations  14.2 us (2%)
    psum x1, waiting for transfers between devices, local(): d_hidden = lax.psum(hidden_part, 'src')  75.2 us
    psum x1, waiting for transfers between devices, local(): x_low = lax.psum(mm(place_low, got_proj), 'src')  64.6 us
    psum x1, waiting for transfers between devices, local(): attn_total = lax.psum(part, 'src')  64.2 us
    psum x1, waiting for transfers between devices, local(): x_high = lax.psum(placed_high, 'src')  59.1 us
    all_to_all x2, blocking collectives, exchange(): return lax.all_to_all(value, axis, split_axis=0, concat_axis=0, tiled=True)  54.3 us
    all_to_all x6, waiting for transfers between devices, exchange(): return lax.all_to_all(value, axis, split_axis=0, concat_axis=0, tiled=True)  41.4 us
    pallas_call x1, Pallas kernels, attend_forward(): pl.pallas_call(forward_kernel, grid_spec=pltpu.PrefetchScalarGridSpec(num...  37.6 us
    pallas_call x1, Pallas kernels, attend_backward(): pl.pallas_call(backward_kernel, grid_spec=pltpu.PrefetchScalarGridSpec(nu...  36.6 us
  transfers between devices with their start and end apart: 16, of which 9 were waited for; matrix products, arithmetic and copies ran while one was open for 9% of the time, Pallas kernels for 8%

profile of v3, /device:TPU:0, one launch (start us, length us, event | category | flops | bytes accessed | tf_op | source)
XLA Modules:
  0.0 602.5 jit_solution(17872321967476261353)
XLA Ops:
  7.2 0.8 multiply_subtract_fusion
  8.0 2.3 reduce-window.6
  10.3 0.3 slice_reduce_fusion
  10.6 0.2 reduce-window.9
  10.9 0.7 add_select_fusion.1
  11.6 7.0 %fusion.12 = bf16[1024,768]{1,0:T(8,128)(2,1)} fusion(s32[1024]{0:T(1024)S(1)} %add_select_fusion.1, bf16[1024,1536]{1,0:T(8,128)(2,1)S(1)} %copy-done, bf16[1536,768]{1,0:T(8,128)(2,1)} %param.10), kind=kOutput, calls=%fused_computation.17 | convolution fusion | flops 4029153280 | bytes 7081984 | tf_op jit(solution)/shard_map/dot_general | solution.py:328
  18.6 5.2 all-to-all-start.1
  23.8 1.2 select_reduce_fusion
  25.0 19.9 %all-to-all-done.1 = bf16[8,128,768]{2,1,0:T(8,128)(2,1)} async-done(((bf16[8,128,768]{2,1,0:T(8,128)(2,1)}), bf16[8,128,768]{2,1,0:T(8,128)(2,1)}, u32[]{:S(2)}, u32[]{:S(2)}) %all-to-all-start.1) | async-done | bytes 1572896 | tf_op jit(solution)/shard_map/all_to_all | solution.py:312
  44.9 3.3 all-to-all-start
  48.2 4.7 fusion.9
  53.0 4.4 all-to-all-start.2
  57.5 4.5 convolution_convert_fusion.1
  62.0 0.2 all-reduce.7.cloned.1.call-start
  62.3 2.0 iota_compare_fusion
  64.3 4.4 convolution_convert_fusion.2
  68.7 64.6 %all-reduce.5.cloned.1.call-done.x_ref = bf16[1024,768]{1,0:T(8,128)(2,1)} async-done(((bf16[1024,768]{1,0:T(8,128)(2,1)}), bf16[1024,768]{1,0:T(8,128)(2,1)}) %all-reduce.5.cloned.1.call-update) | async-done | bytes 1572880 | tf_op jit(solution)/shard_map/psum | solution.py:360
  133.4 3.9 shard_map.119
  137.3 2.2 collective-permute-start
  139.4 1.3 collective-permute-start.1
  140.8 10.3 %fusion.4 = bf16[2048,1536]{1,0:T(8,128)(2,1)} fusion(bf16[1024,1536]{1,0:T(8,128)(2,1)} %bitcast.9, pred[1024,1024]{1,0:T(32,128)(4,1)} %get-tuple-element.72, pred[1024,1024]{1,0:T(32,128)(4,1)S(1)} %get-tuple-element.71), kind=kOutput, calls=%fused_computation.4 | convolution fusion | flops 6447693824 | bytes 11534336 | tf_op jit(solution)/shard_map/dot_general | solution.py:328
  151.2 0.9 copy-done.9
  152.0 59.1 %all-reduce.7.cloned.1.call-done.x_ref = bf16[1024,768]{1,0:T(8,128)(2,1)} async-done(((bf16[1024,768]{1,0:T(8,128)(2,1)}), bf16[1024,768]{1,0:T(8,128)(2,1)}) %all-reduce.7.cloned.1.call-update) | async-done | bytes 1572880 | tf_op jit(solution)/shard_map/psum | solution.py:362
  211.2 4.0 shard_map.120
  215.2 2.2 collective-permute-start.2
  217.6 1.3 collective-permute-start.3
  219.0 1.3 constant_dynamic-update-slice_fusion.7
  220.3 1.2 constant_dynamic-update-slice_fusion.6
  221.9 0.7 collective-permute-done.3
  222.7 2.1 copy-done.11
  224.8 37.6 %shard_map.121 = (bf16[2048,768]{1,0:T(8,128)(2,1)}, bf16[16,4,128,512]{3,2,1,0:T(8,128)(2,1)}, f32[192,768]{1,0:T(8,128)S(1)}) custom-call(s32[64]{0:T(128)S(1)} %reshape.83.index_ref, bf16[16,192,128]{2,1,0:T(8,128)(2,1)S(1)} %constant_dynamic-update-slice_fusion.q_ref, bf16[48,384,128]{2,1,0:T(8,128)(2,1)} %copy-done.11, bf16[192,768]{1,0:T(8,128)(2,1)S(1)} %copy-done.3, ...), custom_call_target="tpu_custom_call" | custom-call | flops 3221225472 | bytes 62914560 | tf_op jit(solution)/shard_map/pallas_call | solution.py:112
  262.6 36.6 %shard_map.122 = (bf16[16,192,128]{2,1,0:T(8,128)(2,1)S(1)}, bf16[16,384,128]{2,1,0:T(8,128)(2,1)}, f32[16,384,128]{2,1,0:T(8,128)}, bf16[16,384,128]{2,1,0:T(8,128)(2,1)}) custom-call(s32[64]{0:T(128)S(1)} %reshape.83.index_ref, bf16[16,192,128]{2,1,0:T(8,128)(2,1)S(1)} %constant_dynamic-update-slice_fusion.q_ref, bf16[48,384,128]{2,1,0:T(8,128)(2,1)} %copy-done.11, ...), custom_call_target="tpu_custom_call" | custom-call | flops 6442450944 | bytes 94371840 | tf_op jit(solution)/shard_map/pallas_call | solution.py:189
  299.1 1.3 collective-permute-start.4
  300.4 17.8 %collective-permute-start.5 = (bf16[16,384,128]{2,1,0:T(8,128)(2,1)}, bf16[16,384,128]{2,1,0:T(8,128)(2,1)S(1)}, u32[]{:S(2)}, u32[]{:S(2)}) collective-permute-start(bf16[16,384,128]{2,1,0:T(8,128)(2,1)} %get-tuple-element.53), channel_id=1, source_target_pairs={{0,1},{1,2},{2,3},{3,4},{4,5},{5,6},{6,7},{8,9},{9,10},{10,11},{11... | collective-permute-start | bytes 4718600 | tf_op jit(solution)/shard_map/ppermute | solution.py:308
  318.3 1.8 pad_maximum_fusion.hid_ref
  320.2 1.0 collective-permute-done.5.left_ref
  321.3 1.0 copy-done.15
  322.3 10.0 %shard_map.123 = (bf16[2048,768]{1,0:T(8,128)(2,1)}, f32[576,768]{1,0:T(8,128)}) custom-call(bf16[16,192,128]{2,1,0:T(8,128)(2,1)S(1)} %get-tuple-element.50.dq_ref, f32[16,384,128]{2,1,0:T(8,128)} %get-tuple-element.51.own_ref, bf16[16,384,128]{2,1,0:T(8,128)(2,1)} %copy-done.14, bf16[16,384,128]{2,1,0:T(8,128)(2,1)} %copy-done.15, ...), custom_call_target="tpu_custom_call" | custom-call | flops 3623878656 | bytes 13369344 | tf_op jit(solution)/shard_map/pallas_call | solution.py:243
  332.4 64.2 %all-reduce.9.cloned.1.call-done = bf16[2048,768]{1,0:T(8,128)(2,1)} async-done(((bf16[2048,768]{1,0:T(8,128)(2,1)}), bf16[2048,768]{1,0:T(8,128)(2,1)}) %all-reduce.9.cloned.1.call-update) | async-done | bytes 3145744 | tf_op jit(solution)/shard_map/psum | solution.py:388
  396.8 20.2 %all_to_all.48 = bf16[8,96,768]{2,1,0:T(8,128)(2,1)S(1)} all-to-all(bf16[8,96,768]{2,1,0:T(8,128)(2,1)S(1)} %bitcast.53), channel_id=1, replica_groups=mesh['src'=4,'ctx'=8] {'ctx'}, dimensions={0} | all-to-all | bytes 2359296 | tf_op jit(solution)/shard_map/all_to_all | solution.py:312
  417.0 0.2 reduce_sum.52
  417.2 1.1 broadcast_in_dim.33
  418.3 4.3 all-to-all-start.4
  422.6 1.7 constant_dynamic-update-slice_fusion.9
  424.2 1.5 constant_dynamic-update-slice_fusion.8.x_ref
  425.8 2.7 add_convert_fusion
  428.5 10.9 %all-to-all-done.4 = bf16[8,96,768]{2,1,0:T(8,128)(2,1)} async-done(((bf16[8,96,768]{2,1,0:T(8,128)(2,1)}), bf16[8,96,768]{2,1,0:T(8,128)(2,1)}, u32[]{:S(2)}, u32[]{:S(2)}) %all-to-all-start.4) | async-done | bytes 1179680 | tf_op jit(solution)/shard_map/all_to_all | solution.py:312
  439.4 2.5 slice.25
  441.9 1.8 slice.26
  443.7 75.2 %all-reduce.11.cloned.1.call-done.dh_ref = bf16[2048,768]{1,0:T(8,128)(2,1)} async-done(((bf16[2048,768]{1,0:T(8,128)(2,1)}), bf16[2048,768]{1,0:T(8,128)(2,1)}) %all-reduce.11.cloned.1.call-update) | async-done | bytes 3145744 | tf_op jit(solution)/shard_map/psum | solution.py:395
  518.9 7.9 %shard_map.124 = (bf16[2048,768]{1,0:T(8,128)(2,1)}, f32[1,768]{1,0:T(1,128)S(1)}) custom-call(bf16[2048,768]{1,0:T(8,128)(2,1)} %all-reduce.11.cloned.1.call-done.dh_ref, bf16[2048,768]{1,0:T(8,128)(2,1)} %copy-done.4, bf16[2048,768]{1,0:T(8,128)(2,1)} %up_ref.5, f32[1,768]{1,0:T(1,128)S(1)} %reshape.87.gain_ref), custom_call_target="tpu_custom_call" | custom-call | flops 47185920 | bytes 12582912 | tf_op jit(solution)/shard_map/pallas_call | solution.py:291
  526.8 0.5 broadcast.47
  527.3 0.7 reduce.6
  528.0 0.6 reshape.95
  528.6 3.7 all-to-all-start.5
  532.3 9.2 %convolution_convert_fusion = bf16[1536,768]{1,0:T(8,128)(2,1)} fusion(bf16[2048,1536]{1,0:T(8,128)(2,1)} %fusion.4, bf16[2048,768]{1,0:T(8,128)(2,1)} %get-tuple-element.65), kind=kOutput, calls=%fused_computation.12 | convolution fusion | flops 4833017856 | bytes 11796480 | tf_op jit(solution)/shard_map/dot_general | solution.py:19
  541.6 34.1 %all_to_all.49 = bf16[8,192,768]{2,1,0:T(8,128)(2,1)} all-to-all(bf16[8,192,768]{2,1,0:T(8,128)(2,1)} %bitcast.55), channel_id=1, replica_groups=mesh['src'=4,'ctx'=8] {'ctx'}, dimensions={0} | all-to-all | bytes 4718592 | tf_op jit(solution)/shard_map/all_to_all | solution.py:312
  575.7 2.8 reduce_sum.53
  578.4 1.3 convert_element_type.87
  579.8 0.8 copy.19
  580.6 3.5 all-to-all-start.7
  584.0 0.6 convert_reduce_fusion.1
  584.6 10.6 %all-to-all-done.7 = bf16[4,192,192]{2,1,0:T(8,128)(2,1)S(1)} async-done(((bf16[4,192,192]{2,1,0:T(8,128)(2,1)}), bf16[4,192,192]{2,1,0:T(8,128)(2,1)S(1)}, u32[]{:S(2)}, u32[]{:S(2)}) %all-to-all-start.7) | async-done | bytes 294944 | tf_op jit(solution)/shard_map/all_to_all | solution.py:312
  595.3 0.7 convert_reduce_fusion
  (64 shorter events, 1.6 us)
Async XLA Ops:
  7.2 4.4 copy-start
  18.6 26.3 %all-to-all-start.1 = ((bf16[8,128,768]{2,1,0:T(8,128)(2,1)}), bf16[8,128,768]{2,1,0:T(8,128)(2,1)}, u32[]{:S(2)}, u32[]{:S(2)}) async-start(bf16[8,128,768]{2,1,0:T(8,128)(2,1)} %bitcast.57), calls=%async_computation.1 | async-start | bytes 3145728 | tf_op jit(solution)/shard_map/all_to_all | solution.py:312
  44.9 8.1 %all-to-all-start = ((s32[8,1,128]{2,1,0:T(1,128)}), s32[8,1,128]{2,1,0:T(1,128)S(1)}, u32[]{:S(2)}, u32[]{:S(2)}) async-start(s32[8,1,128]{2,1,0:T(1,128)} %bitcast.2), calls=%async_computation | async-start | bytes 8192 | tf_op jit(solution)/shard_map/all_to_all | solution.py:312
  53.0 87.8 %all-to-all-start.2 = ((bf16[8,128,1536]{2,1,0:T(8,128)(2,1)}), bf16[8,128,1536]{2,1,0:T(8,128)(2,1)}, u32[]{:S(2)}, u32[]{:S(2)}) async-start(bf16[8,128,1536]{2,1,0:T(8,128)(2,1)} %bitcast.54), calls=%async_computation.2 | async-start | bytes 6291456 | tf_op jit(solution)/shard_map/all_to_all | solution.py:312
  57.4 75.9 %all-reduce.5.cloned.1.call-start = ((), (), s32[]{:S(2)}) async-start(), calls=%async_computation.8 | async-start | bytes 3145728 | tf_op jit(solution)/shard_map/psum | solution.py:360
  57.5 4.8 copy-start.12
  62.0 149.2 %all-reduce.7.cloned.1.call-start = ((), (), s32[]{:S(2)}) async-start(), calls=%async_computation.9 | async-start | bytes 3145728 | tf_op jit(solution)/shard_map/psum | solution.py:362
  137.3 13.9 %collective-permute-start = (bf16[8,384,128]{2,1,0:T(8,128)(2,1)S(1)}, bf16[8,384,128]{2,1,0:T(8,128)(2,1)}, u32[]{:S(2)}, u32[]{:S(2)}) collective-permute-start(bf16[8,384,128]{2,1,0:T(8,128)(2,1)S(1)} %get-tuple-element.43), channel_id=1, source_target_pairs={{0,1},{1,2},{2,3},{3,4},{4,5},{5,6},{6,7},{8,9},{9,10},{10,11},{11... | collective-permute-start | bytes 2359304 | tf_op jit(solution)/shard_map/ppermute | solution.py:308
  139.4 11.7 %collective-permute-start.1 = (bf16[8,384,128]{2,1,0:T(8,128)(2,1)S(1)}, bf16[8,384,128]{2,1,0:T(8,128)(2,1)S(1)}, u32[]{:S(2)}, u32[]{:S(2)}) collective-permute-start(bf16[8,384,128]{2,1,0:T(8,128)(2,1)S(1)} %get-tuple-element.43), channel_id=1, source_target_pairs={{1,0},{2,1},{3,2},{4,3},{5,4},{6,5},{7,6},{9,8},{10,9},{11,10},{12... | collective-permute-start | bytes 2359304 | tf_op jit(solution)/shard_map/ppermute | solution.py:308
  140.7 255.8 %all-reduce.9.cloned.1.call-start = ((), (), s32[]{:S(2)}) async-start(), calls=%async_computation.10 | async-start | bytes 6291456 | tf_op jit(solution)/shard_map/psum | solution.py:388
  151.1 66.2 %copy-start.13 = (s32[128,4]{0,1:T(4,128)S(1)}, s32[128,4]{0,1:T(4,128)}, u32[]{:S(2)}) copy-start(s32[128,4]{0,1:T(4,128)} %param.14) | copy-start | bytes 6148
  151.2 0.9 copy-start.9
  215.2 5.1 collective-permute-start.2
  217.6 5.0 collective-permute-start.3
  219.0 2.8 copy-start.10
  221.5 3.3 copy-start.3
  222.7 2.1 copy-start.11
  262.5 256.4 %all-reduce.11.cloned.1.call-start = ((), (), s32[]{:S(2)}) async-start(), calls=%async_computation.11 | async-start | bytes 6291456 | tf_op jit(solution)/shard_map/psum | solution.py:395
  262.5 55.7 %copy-start.7 = (bf16[1024,768]{1,0:T(8,128)(2,1)S(1)}, bf16[1024,768]{1,0:T(8,128)(2,1)}, u32[]{:S(2)}) copy-start(bf16[1024,768]{1,0:T(8,128)(2,1)} %get-tuple-element.54) | copy-start | bytes 4718596
  262.5 55.7 %copy-start.8 = (bf16[1024,768]{1,0:T(8,128)(2,1)S(1)}, bf16[1024,768]{1,0:T(8,128)(2,1)}, u32[]{:S(2)}) copy-start(bf16[1024,768]{1,0:T(8,128)(2,1)} %get-tuple-element.55) | copy-start | bytes 4718596
  299.1 21.0 %collective-permute-start.4 = (bf16[16,384,128]{2,1,0:T(8,128)(2,1)}, bf16[16,384,128]{2,1,0:T(8,128)(2,1)S(1)}, u32[]{:S(2)}, u32[]{:S(2)}) collective-permute-start(bf16[16,384,128]{2,1,0:T(8,128)(2,1)} %get-tuple-element.52), channel_id=1, source_target_pairs={{1,0},{2,1},{3,2},{4,3},{5,4},{6,5},{7,6},{9,8},{10,9},{11,10},{12... | collective-permute-start | bytes 4718600 | tf_op jit(solution)/shard_map/ppermute | solution.py:308
  300.4 20.7 %collective-permute-start.5 = (bf16[16,384,128]{2,1,0:T(8,128)(2,1)}, bf16[16,384,128]{2,1,0:T(8,128)(2,1)S(1)}, u32[]{:S(2)}, u32[]{:S(2)}) collective-permute-start(bf16[16,384,128]{2,1,0:T(8,128)(2,1)} %get-tuple-element.53), channel_id=1, source_target_pairs={{0,1},{1,2},{2,3},{3,4},{4,5},{5,6},{6,7},{8,9},{9,10},{10,11},{11... | collective-permute-start | bytes 4718600 | tf_op jit(solution)/shard_map/ppermute | solution.py:308
  318.3 4.1 copy-start.2
  320.2 1.2 copy-start.14
  321.2 1.2 copy-start.15
  332.4 64.2 %copy-start.6 = (f32[576,768]{1,0:T(8,128)S(1)}, f32[576,768]{1,0:T(8,128)}, u32[]{:S(2)}) copy-start(f32[576,768]{1,0:T(8,128)} %get-tuple-element.59) | copy-start | bytes 5308420
  418.3 21.1 %all-to-all-start.4 = ((bf16[8,96,768]{2,1,0:T(8,128)(2,1)}), bf16[8,96,768]{2,1,0:T(8,128)(2,1)}, u32[]{:S(2)}, u32[]{:S(2)}) async-start(bf16[8,96,768]{2,1,0:T(8,128)(2,1)} %broadcast_in_dim.33), calls=%async_computation.4 | async-start | bytes 2359296 | tf_op jit(solution)/shard_map/all_to_all | solution.py:312
  422.6 3.2 copy-start.5
  425.8 2.7 copy-start.4
  528.6 12.9 %all-to-all-start.5 = ((bf16[8,2,384]{2,1,0:T(2,128)(2,1)}), bf16[8,2,384]{2,1,0:T(2,128)(2,1)S(1)}, u32[]{:S(2)}, u32[]{:S(2)}) async-start(bf16[8,2,384]{2,1,0:T(2,128)(2,1)} %reshape.95), calls=%async_computation.5 | async-start | bytes 24576 | tf_op jit(solution)/shard_map/all_to_all | solution.py:312
  541.6 54.4 %copy-start.1 = (bf16[1024,1536]{1,0:T(8,128)(2,1)S(1)}, bf16[1024,1536]{1,0:T(8,128)(2,1)}, u32[]{:S(2)}) copy-start(bf16[1024,1536]{1,0:T(8,128)(2,1)} %param.8) | copy-start | bytes 9437188
  580.6 14.7 %all-to-all-start.7 = ((bf16[4,192,192]{2,1,0:T(8,128)(2,1)}), bf16[4,192,192]{2,1,0:T(8,128)(2,1)S(1)}, u32[]{:S(2)}, u32[]{:S(2)}) async-start(bf16[4,192,192]{2,1,0:T(8,128)(2,1)} %copy.19), calls=%async_computation.7 | async-start | bytes 786432 | tf_op jit(solution)/shard_map/all_to_all | solution.py:312
Sparse Core Ops, SparseCore 0:
  62.1 71.1 all-reduce.4
  140.9 70.2 all-reduce.6
  262.6 133.8 all-reduce.8
  398.8 120.0 all-reduce.10
